TPU v7x, 32 devices: a whole 2x2x4 slice. The times are simulated.
32 devices in a mesh: energy: 4 (over x, core), atom: 8 (over z, y).
Axes of the slice: x: 2, y: 2, z: 4, core: 2. Of those that a mesh axis runs over, the one named last changes fastest.
Arguments:
- green: float32 [2, 8, 16, 128, 128], P(None, 'energy', 'atom'), may hold values from -6 to 6
- coupling: float32 [16, 6, 128, 128], P('atom'), may hold values from -0.5 to 0.5
- phonon: float32 [16, 6, 4], P('atom'), may hold values from 0.2 to 2
- neighbours: int32 [16, 6], P('atom'), may hold values from 0 to 15, as said below
Outputs:
- self_energy: float32 [2, 8, 16, 128, 128], P(None, 'energy', 'atom')
- rates: float32 [16, 128], P('atom')
Inputs may be any that keep to these rules, and one draw needn't show every extreme that they name: `neighbours`: each entry lies within 2 of its row's index and within 0 to 15; offsets +2 and -2 both occur.
All inputs are finite; a program needn't handle non-finite values.
Results may differ from a plain program's by a relative error of at most 0.000071.
Values sent between devices are 32-bit elements; how exact they have to be, the bound alone decides.
No kernel may reach another device: no remote copies, remote signals or barrier semaphores. Data moves between devices by JAX's collectives and lax.ppermute only.
A program may use at most 64 MiB of HBM per device.

v0:
```python
import functools

import jax
import jax.numpy as jnp
from jax import lax
from jax.experimental import pallas as pl
from jax.experimental.pallas import tpu as pltpu
from jax.sharding import PartitionSpec as P

SHIFTS = (-2, -1, 1, 2)
REACH = max(SHIFTS)
OWN, PAIR, FAR = 0, 1, 2
FEW = 4
VMEM = pl.BlockSpec(memory_space=pltpu.VMEM)
SMEM = pl.BlockSpec(memory_space=pltpu.SMEM)
ANY = pl.BlockSpec(memory_space=pl.ANY)


def halves(x):
    high = x.astype(jnp.bfloat16)
    return high, (x - high.astype(jnp.float32)).astype(jnp.bfloat16)


def swap(x, axis, first, close=False):
    size = lax.axis_size(axis)
    pairs = [(i, i + 1) for i in range(first, size - 1, 2)]
    if close and first == 1 and size % 2 == 0:
        pairs.append((0, size - 1))
    return lax.ppermute(x, axis, pairs + [(j, i) for i, j in pairs])


def forward(x, axis):
    size = lax.axis_size(axis)
    ups = [(i, i + 2) for i in range(0, size - 2, 2)]
    downs = [(i + 2, i) for i in range(1, size - 2, 2)]
    return lax.ppermute(x, axis, ups + downs)


def put_blocks(blocks, c, green):
    orb = green.shape[-1]
    for e in range(green.shape[0]):
        for a in range(green.shape[1]):
            high, low = halves(green[e, a])
            blocks[c, a, e, :, :orb] = high
            blocks[c, a, e, :, orb:] = low


def add_pairs(group, neighbours, phonon, coupling, blocks, totals, picked, size):
    atoms, slots, orb = coupling.shape[0], coupling.shape[1], coupling.shape[-1]
    e_local = blocks.shape[2]
    index = lax.axis_index("atom")
    base = index * atoms
    if group != OWN:
        upper = (index & 1) == (0 if group == PAIR else 1)
        base += jnp.where(upper, atoms, -atoms)

    found = jnp.int32(0)
    for a in range(atoms):
        for j in range(slots):
            picked[found] = a * slots + j
            b = neighbours[a, j] - base
            found += ((b >= 0) & (b < atoms)).astype(jnp.int32)

    def batch(step, _):
        pairs = []
        for u in range(size):
            at = step * size + u
            item = picked[jnp.minimum(at, found - 1)]
            a = item // slots
            j = item - a * slots
            high, low = halves(coupling[a, j])
            left = jnp.concatenate([high, low], 1)
            right = jnp.concatenate(
                [jnp.concatenate([high, high], 1), jnp.concatenate([low, low], 1)], 0
            )
            pairs.append((a, j, neighbours[a, j] - base, jnp.where(at < found, 1.0, 0.0), left, right))
        inners = []
        for a, j, b, live, left, right in pairs:
            for c in range(len(totals)):
                near = blocks[c, b].reshape(e_local * orb, 2 * orb)
                inner = lax.dot_general(
                    near, right, (((1,), (1,)), ((), ())), preferred_element_type=jnp.float32
                )
                inners.append(inner[:, :orb] + inner[:, orb:])
        results = []
        for a, j, b, live, left, right in pairs:
            for total in totals:
                inner = inners.pop(0)
                sums = [None] * (e_local + 2 * REACH)
                for e in range(e_local):
                    high, low = halves(inner[e * orb : (e + 1) * orb])
                    both = jnp.concatenate([high, low], 1)
                    outer = jnp.dot(
                        left, jnp.concatenate([both, both], 0), preferred_element_type=jnp.float32
                    )
                    outer = outer[:, :orb] + outer[:, orb:]
                    for k, s in enumerate(SHIFTS):
                        d = e - s + REACH
                        term = (phonon[a, k, j] * live) * outer
                        sums[d] = term if sums[d] is None else sums[d] + term
                results.append((total, a, sums))
        for total, a, sums in results:
            for d, value in enumerate(sums):
                if value is not None:
                    total[d, a] += value

    lax.fori_loop(0, (found + size - 1) // size, batch, None)


def fetch_kernel(green, coupling, phonon, neighbours, *rest):
    *results, sems = rest
    sources = [green.at[0], green.at[1], green, coupling, phonon, neighbours]
    copies = [
        pltpu.make_async_copy(source, result, sems.at[i])
        for i, (source, result) in enumerate(zip(sources, results))
    ]
    for copy in copies:
        copy.start()
    for copy in copies:
        copy.wait()


def own_kernel(neighbours, phonon, coupling, green0, green1, total0, total1, blocks, picked):
    for c, (green, total) in enumerate(((green0, total0), (green1, total1))):
        put_blocks(blocks, c, green)
        total[...] = jnp.zeros_like(total)
    add_pairs(OWN, neighbours, phonon, coupling, blocks, (total0, total1), picked, 2)


def pair_kernel(
    size, neighbours, phonon, coupling, ahead0, ahead1, before0, before1, green, by_core, by_cross,
    total0, total1, turned, blocks, picked,
):
    e_local, a_local = green.shape[1], green.shape[2]
    core, cross = partner_energies(turned.shape[1])
    has_core, has_cross = has_partners(size)
    for c in range(2):
        for a in range(a_local):
            for e in range(e_local):
                turned[c, REACH + e, a] = green[c, e, a].T
            for e in range(REACH):
                turned[c, core + e, a] = by_core[c, e, a].T * has_core
                turned[c, cross + e, a] = by_cross[c, e, a].T * has_cross
    total0[...] = before0[...]
    total1[...] = before1[...]
    put_blocks(blocks, 0, ahead0)
    put_blocks(blocks, 1, ahead1)
    add_pairs(PAIR, neighbours, phonon, coupling, blocks, (total0, total1), picked, 2)


def partner_energies(spread):
    odd = lax.axis_index("energy") & 1
    return jnp.where(odd == 0, spread - REACH, 0), jnp.where(odd == 0, 0, spread - REACH)


def has_partners(size):
    me = lax.axis_index("energy")
    above, below = jnp.where(me < size - 1, 1.0, 0.0), jnp.where(me > 0, 1.0, 0.0)
    odd = me & 1
    return jnp.where(odd == 0, above, below), jnp.where(odd == 0, below, above)


def finish(total, core, cross):
    to_core, to_cross = partner_energies(total.shape[0])
    for e in range(REACH):
        core[e] = total[to_core + e]
        cross[e] = total[to_cross + e]


def rate_sums(total, turned, c, a):
    sums = total[0, a] * turned[c, 0, a]
    for d in range(1, total.shape[0]):
        sums += total[d, a] * turned[c, d, a]
    return sums


def far_kernel(
    neighbours, phonon, coupling, across, before, turned, total, core, cross, partial, blocks, picked
):
    add_far(neighbours, phonon, coupling, across, before, total, blocks, picked)
    finish(total, core, cross)
    for a in range(partial.shape[0]):
        partial[a] = rate_sums(total, turned, 0, a)


def add_far(neighbours, phonon, coupling, across, before, total, blocks, picked):
    total[...] = before[...]
    put_blocks(blocks, 0, across)
    add_pairs(FAR, neighbours, phonon, coupling, blocks, (total,), picked, 4)


def last_kernel(
    scale, neighbours, phonon, coupling, across, before, turned, partial,
    total, core, cross, rate, blocks, picked,
):
    add_far(neighbours, phonon, coupling, across, before, total, blocks, picked)
    finish(total, core, cross)
    for a in range(partial.shape[0]):
        sums = partial[a] - rate_sums(total, turned, 1, a)
        rate[a : a + 1, :] = jnp.sum(sums.T, axis=0, keepdims=True) * scale


def addends(x, axis):
    size = lax.axis_size(axis)
    if size > FEW:
        return [lax.psum(x, axis)]
    turns = [[(i, (i + k) % size) for i in range(size)] for k in range(1, size)]
    return [x] + [lax.ppermute(x, axis, turn) for turn in turns]


def end_kernel(size, total0, total1, cross0, core0, cross1, core1, *rest):
    *rates, out, rate = rest
    e_local = out.shape[1]
    has_core, has_cross = has_partners(size)
    for c, (total, cross, core) in enumerate(((total0, cross0, core0), (total1, cross1, core1))):
        for e in range(e_local):
            out[c, e] = total[REACH + e] + core[e] * has_core + cross[e] * has_cross
    rate[...] = sum(r[...] for r in rates)


def per_device(green, coupling, phonon, neighbours):
    _, e_local, a_local, orb, _ = green.shape
    energies = lax.axis_size("energy")
    points = e_local * energies
    spread = (e_local + 2 * REACH, a_local, orb, orb)
    edge = (REACH, a_local, orb, orb)

    def call(kernel, out, operands, parts=1):
        return pl.pallas_call(
            kernel,
            out_shape=[jax.ShapeDtypeStruct(shape, jnp.float32) for shape in out],
            in_specs=[SMEM, SMEM] + [VMEM] * (1 + len(operands)),
            out_specs=[VMEM] * len(out),
            scratch_shapes=[
                pltpu.VMEM((parts, a_local, e_local, orb, 2 * orb), jnp.bfloat16),
                pltpu.SMEM((a_local * neighbours.shape[1] + 1,), jnp.int32),
            ],
            compiler_params=pltpu.CompilerParams(vmem_limit_bytes=24 * 2**20),
            cost_estimate=pl.CostEstimate(flops=10**6, bytes_accessed=10**4, transcendentals=0),
        )(neighbours, phonon, coupling, *operands)

    sources = (green, coupling, jnp.swapaxes(phonon, 1, 2), neighbours)
    green0, green1, green, coupling, phonon, neighbours = pl.pallas_call(
        fetch_kernel,
        out_shape=[jax.ShapeDtypeStruct(green.shape[1:], green.dtype)] * 2
        + [jax.ShapeDtypeStruct(x.shape, x.dtype) for x in sources],
        in_specs=[ANY] * 4,
        out_specs=[VMEM] * 6,
        scratch_shapes=[pltpu.SemaphoreType.DMA((6,))],
        compiler_params=pltpu.CompilerParams(vmem_limit_bytes=24 * 2**20),
    )(*(pltpu.with_memory_space_constraint(x, pltpu.HBM) for x in sources))
    ahead1 = swap(green1, "atom", 0)
    ahead0 = swap(green0, "atom", 0)
    by_core, by_cross = swap(green, "energy", 0), swap(green, "energy", 1, close=True)
    total0, total1 = call(own_kernel, [spread] * 2, (green0, green1), parts=2)
    ahead0, total0, total1 = lax.optimization_barrier((ahead0, total0, total1))
    across0 = forward(ahead0, "atom")
    green1, ahead0 = lax.optimization_barrier((green1, ahead0))
    across1 = swap(green1, "atom", 1)
    total0, total1, turned = call(
        functools.partial(pair_kernel, energies),
        [spread, spread, (2,) + spread],
        (ahead0, ahead1, total0, total1, green, by_core, by_cross),
        parts=2,
    )
    total0, core0, cross0, partial = call(
        far_kernel, [spread, edge, edge, (a_local, orb, orb)], (across0, total0, turned)
    )
    core0, cross0 = swap(core0, "energy", 0), swap(cross0, "energy", 1, close=True)
    total1, core1, cross1, rate = call(
        functools.partial(last_kernel, 1.0 / (4.0 * points)),
        [spread, edge, edge, (a_local, orb)],
        (across1, total1, turned, partial),
    )
    core1, cross1 = swap(core1, "energy", 0), swap(cross1, "energy", 1)
    cross0, core0, rate = lax.optimization_barrier((cross0, core0, rate))
    rates = addends(rate, "energy")
    return pl.pallas_call(
        functools.partial(end_kernel, energies),
        out_shape=[
            jax.ShapeDtypeStruct(green.shape, jnp.float32),
            jax.ShapeDtypeStruct((a_local, orb), jnp.float32),
        ],
        in_specs=[VMEM] * (6 + len(rates)),
        out_specs=[VMEM] * 2,
        compiler_params=pltpu.CompilerParams(vmem_limit_bytes=24 * 2**20),
        cost_estimate=pl.CostEstimate(flops=10**6, bytes_accessed=2 * 10**6, transcendentals=0),
    )(total0, total1, cross0, core0, cross1, core1, *rates)


def solution(mesh):
    return jax.shard_map(
        per_device,
        mesh=mesh,
        in_specs=(
            P(None, "energy", "atom", None, None),
            P("atom", None, None, None),
            P("atom", None, None),
            P("atom", None),
        ),
        out_specs=(P(None, "energy", "atom", None, None), P("atom", None)),
        check_vma=False,
    )
```

profile of v0, /device:TPU:0, one launch (start us, length us, event | category | flops | bytes accessed | tf_op | source)
XLA Modules:
  0.0 38.1 jit_solution(10567943405260232675)
XLA Ops:
  0.6 1.5 %shard_map.59 = (f32[2,2,128,128]{3,2,1,0:T(8,128)S(1)}, f32[2,2,128,128]{3,2,1,0:T(8,128)S(1)}, f32[2,2,2,128,128]{4,3,2,1,0:T(8,128)S(1)}, f32[2,6,128,128]{3,...) custom-call(f32[2,2,2,128,128]{4,3,2,1,0:T(8,128)} %green.1, f32[2,6,128,128]{3,2,1,0:T(8,128)} %coupling.1, ...), custom_call_target="tpu_custom_call" | custom-call | tf_op jit(solution)/shard_map/pallas_call | solution.py:243
  2.2 3.0 %collective-permute-start = (f32[2,2,128,128]{3,2,1,0:T(8,128)S(1)}, f32[2,2,128,128]{3,2,1,0:T(8,128)S(1)}, u32[]{:S(2)}, u32[]{:S(2)}) collective-permute-start(f32[2,2,128,128]{3,2,1,0:T(8,128)S(1)} %get-tuple-element.32.green0), channel_id=1, source_target_pairs={{0,1},{2,3},{4,5},{6,7},{1,0},{3,2},{5,4},{7,6},{8,9},{10,11},{12,... | collective-permute-start | bytes 786440 | tf_op jit(solution)/shard_map/ppermute | solution.py:29
  5.2 0.7 %collective-permute-start.4 = (f32[2,2,2,128,128]{4,3,2,1,0:T(8,128)S(1)}, f32[2,2,2,128,128]{4,3,2,1,0:T(8,128)S(1)}, u32[]{:S(2)}, u32[]{:S(2)}) collective-permute-start(f32[2,2,2,128,128]{4,3,2,1,0:T(8,128)S(1)} %get-tuple-element.40.green), channel_id=1, source_target_pairs={{8,16},{0,24},{16,8},{24,0},{9,17},{1,25},{17,9},{25,1},{10,18},{2... | collective-permute-start | bytes 1572872 | tf_op jit(solution)/shard_map/ppermute | solution.py:29
  5.8 1.0 %collective-permute-start.3 = (f32[2,2,2,128,128]{4,3,2,1,0:T(8,128)S(1)}, f32[2,2,2,128,128]{4,3,2,1,0:T(8,128)S(1)}, u32[]{:S(2)}, u32[]{:S(2)}) collective-permute-start(f32[2,2,2,128,128]{4,3,2,1,0:T(8,128)S(1)} %get-tuple-element.40.green), channel_id=1, source_target_pairs={{0,8},{16,24},{8,0},{24,16},{1,9},{17,25},{9,1},{25,17},{2,10},{18... | collective-permute-start | bytes 1572872 | tf_op jit(solution)/shard_map/ppermute | solution.py:29
  6.8 0.5 %collective-permute-start.2 = (f32[2,2,128,128]{3,2,1,0:T(8,128)S(1)}, f32[2,2,128,128]{3,2,1,0:T(8,128)S(1)}, u32[]{:S(2)}, u32[]{:S(2)}) collective-permute-start(f32[2,2,128,128]{3,2,1,0:T(8,128)S(1)} %get-tuple-element.44.green1), channel_id=1, source_target_pairs={{0,1},{2,3},{4,5},{6,7},{1,0},{3,2},{5,4},{7,6},{8,9},{10,11},{12,... | collective-permute-start | bytes 786440 | tf_op jit(solution)/shard_map/ppermute | solution.py:29
  7.3 2.0 %shard_map.60 = (f32[6,2,128,128]{3,2,1,0:T(8,128)S(1)}, f32[6,2,128,128]{3,2,1,0:T(8,128)S(1)}) custom-call(s32[2,6]{1,0:T(2,128)S(1)} %get-tuple-element.29.neighbours, f32[2,4,6]{2,1,0:T(4,128)S(1)} %get-tuple-element.30.phonon, f32[2,6,128,128]{3,2,1,0:T(8,128)S(1)} %get-tuple-element.31.coupling, f32[2,2,128,128]{3,2,1,0:T(8,128)S(1)} %get-tuple-element.32.green0, ...), custom_call_target="tpu_custom_call" | custom-call | flops 1000000 | bytes 10000 | tf_op jit(solution)/shard_map/pallas_call | solution.py:229
  9.3 3.0 %collective-permute-done.ahead0 = f32[2,2,128,128]{3,2,1,0:T(8,128)S(1)} collective-permute-done((f32[2,2,128,128]{3,2,1,0:T(8,128)S(1)}, f32[2,2,128,128]{3,2,1,0:T(8,128)S(1)}, u32[]{:S(2)}, u32[]{:S(2)}) %collective-permute-start) | collective-permute-done | bytes 262176 | tf_op jit(solution)/shard_map/ppermute | solution.py:29
  12.3 4.0 %collective-permute-start.1 = (f32[2,2,128,128]{3,2,1,0:T(8,128)S(1)}, f32[2,2,128,128]{3,2,1,0:T(8,128)S(1)}, u32[]{:S(2)}, u32[]{:S(2)}) collective-permute-start(f32[2,2,128,128]{3,2,1,0:T(8,128)S(1)} %collective-permute-done.ahead0), channel_id=1, source_target_pairs={{0,2},{2,4},{4,6},{3,1},{5,3},{7,5},{8,10},{10,12},{12,14},{11,9},... | collective-permute-start | bytes 786440 | tf_op jit(solution)/shard_map/ppermute | solution.py:36
  16.3 0.7 %collective-permute-start.5 = (f32[2,2,128,128]{3,2,1,0:T(8,128)S(1)}, f32[2,2,128,128]{3,2,1,0:T(8,128)S(1)}, u32[]{:S(2)}, u32[]{:S(2)}) collective-permute-start(f32[2,2,128,128]{3,2,1,0:T(8,128)S(1)} %get-tuple-element.44.green1), channel_id=1, source_target_pairs={{1,2},{3,4},{5,6},{2,1},{4,3},{6,5},{9,10},{11,12},{13,14},{10,9},... | collective-permute-start | bytes 786440 | tf_op jit(solution)/shard_map/ppermute | solution.py:29
  17.0 0.1 collective-permute-done.2.ahead1
  17.1 2.3 %collective-permute-done.4.by_cross = f32[2,2,2,128,128]{4,3,2,1,0:T(8,128)S(1)} collective-permute-done((f32[2,2,2,128,128]{4,3,2,1,0:T(8,128)S(1)}, f32[2,2,2,128,128]{4,3,2,1,0:T(8,128)S(1)}, u32[]{:S(2)}, u32[]{:S(2)}) %collective-permute-start.4) | collective-permute-done | bytes 524320 | tf_op jit(solution)/shard_map/ppermute | solution.py:29
  19.4 0.0 collective-permute-done.3.by_core
  19.4 3.6 %shard_map.61 = (f32[6,2,128,128]{3,2,1,0:T(8,128)S(1)}, f32[6,2,128,128]{3,2,1,0:T(8,128)S(1)}, f32[2,6,2,128,128]{4,3,2,1,0:T(8,128)S(1)}) custom-call(s32[2,6]{1,0:T(2,128)S(1)} %get-tuple-element.29.neighbours, f32[2,4,6]{2,1,0:T(4,128)S(1)} %get-tuple-element.30.phonon, f32[2,6,128,128]{3,2,1,0:T(8,128)S(1)} %get-tuple-element.31.coupling, ...), custom_call_target="tpu_custom_call" | custom-call | flops 1000000 | bytes 10000 | tf_op jit(solution)/shard_map/pallas_call | solution.py:229
  23.0 0.0 collective-permute-done.1.across
  23.0 0.9 %shard_map.62 = (f32[6,2,128,128]{3,2,1,0:T(8,128)S(1)}, f32[2,2,128,128]{3,2,1,0:T(8,128)S(1)}, f32[2,2,128,128]{3,2,1,0:T(8,128)S(1)}, f32[2,128,128]{2,1,0:T(8,128)S(1)}) custom-call(s32[2,6]{1,0:T(2,128)S(1)} %get-tuple-element.29.neighbours, f32[2,4,6]{2,1,0:T(4,128)S(1)} %get-tuple-element.30.phonon, ...), custom_call_target="tpu_custom_call" | custom-call | flops 1000000 | bytes 10000 | tf_op jit(solution)/shard_map/pallas_call | solution.py:229
  23.9 0.8 %collective-permute-start.6 = (f32[2,2,128,128]{3,2,1,0:T(8,128)S(1)}, f32[2,2,128,128]{3,2,1,0:T(8,128)S(1)}, u32[]{:S(2)}, u32[]{:S(2)}) collective-permute-start(f32[2,2,128,128]{3,2,1,0:T(8,128)S(1)} %get-tuple-element.48), channel_id=1, source_target_pairs={{8,16},{0,24},{16,8},{24,0},{9,17},{1,25},{17,9},{25,1},{10,18},{2... | collective-permute-start | bytes 786440 | tf_op jit(solution)/shard_map/ppermute | solution.py:29
  24.7 0.6 %collective-permute-start.7 = (f32[2,2,128,128]{3,2,1,0:T(8,128)S(1)}, f32[2,2,128,128]{3,2,1,0:T(8,128)S(1)}, u32[]{:S(2)}, u32[]{:S(2)}) collective-permute-start(f32[2,2,128,128]{3,2,1,0:T(8,128)S(1)} %get-tuple-element.49), channel_id=1, source_target_pairs={{0,8},{16,24},{8,0},{24,16},{1,9},{17,25},{9,1},{25,17},{2,10},{18... | collective-permute-start | bytes 786440 | tf_op jit(solution)/shard_map/ppermute | solution.py:29
  25.3 0.0 collective-permute-done.5.across
  25.3 0.9 %shard_map.63 = (f32[6,2,128,128]{3,2,1,0:T(8,128)S(1)}, f32[2,2,128,128]{3,2,1,0:T(8,128)S(1)}, f32[2,2,128,128]{3,2,1,0:T(8,128)S(1)}, f32[2,128]{1,0:T(2,128)S(1)}) custom-call(s32[2,6]{1,0:T(2,128)S(1)} %get-tuple-element.29.neighbours, f32[2,4,6]{2,1,0:T(4,128)S(1)} %get-tuple-element.30.phonon, f32[2,6,128,128]{3,2,1,0:T(8,128)S(1)} %get-tuple-element.31.coupling, ...), custom_call_target="tpu_custom_call" | custom-call | flops 1000000 | bytes 10000 | tf_op jit(solution)/shard_map/pallas_call | solution.py:229
  26.2 0.7 %collective-permute-start.8 = (f32[2,2,128,128]{3,2,1,0:T(8,128)S(1)}, f32[2,2,128,128]{3,2,1,0:T(8,128)S(1)}, u32[]{:S(2)}, u32[]{:S(2)}) collective-permute-start(f32[2,2,128,128]{3,2,1,0:T(8,128)S(1)} %get-tuple-element.53), channel_id=1, source_target_pairs={{8,16},{16,8},{9,17},{17,9},{10,18},{18,10},{11,19},{19,11},{12,20... | collective-permute-start | bytes 786440 | tf_op jit(solution)/shard_map/ppermute | solution.py:29
  26.9 2.2 %collective-permute-start.9 = (f32[2,2,128,128]{3,2,1,0:T(8,128)S(1)}, f32[2,2,128,128]{3,2,1,0:T(8,128)S(1)}, u32[]{:S(2)}, u32[]{:S(2)}) collective-permute-start(f32[2,2,128,128]{3,2,1,0:T(8,128)S(1)} %get-tuple-element.54), channel_id=1, source_target_pairs={{0,8},{16,24},{8,0},{24,16},{1,9},{17,25},{9,1},{25,17},{2,10},{18... | collective-permute-start | bytes 786440 | tf_op jit(solution)/shard_map/ppermute | solution.py:29
  29.1 3.2 %collective-permute-done.6.cross0 = f32[2,2,128,128]{3,2,1,0:T(8,128)S(1)} collective-permute-done((f32[2,2,128,128]{3,2,1,0:T(8,128)S(1)}, f32[2,2,128,128]{3,2,1,0:T(8,128)S(1)}, u32[]{:S(2)}, u32[]{:S(2)}) %collective-permute-start.6) | collective-permute-done | bytes 262176 | tf_op jit(solution)/shard_map/ppermute | solution.py:29
  32.3 0.0 collective-permute-done.7.core0
  32.3 1.3 %collective-permute-start.12 = (f32[2,128]{1,0:T(2,128)S(1)}, f32[2,128]{1,0:T(2,128)S(1)}, u32[]{:S(2)}, u32[]{:S(2)}) collective-permute-start(f32[2,128]{1,0:T(2,128)S(1)} %get-tuple-element.55.rest_0_), channel_id=1, source_target_pairs={{0,24},{8,0},{16,8},{24,16},{1,25},{9,1},{17,9},{25,17},{2,26},{10... | collective-permute-start | bytes 3080 | tf_op jit(solution)/shard_map/ppermute | solution.py:208
  33.6 0.4 %collective-permute-start.11 = (f32[2,128]{1,0:T(2,128)S(1)}, f32[2,128]{1,0:T(2,128)S(1)}, u32[]{:S(2)}, u32[]{:S(2)}) collective-permute-start(f32[2,128]{1,0:T(2,128)S(1)} %get-tuple-element.55.rest_0_), channel_id=1, source_target_pairs={{0,16},{8,24},{16,0},{24,8},{1,17},{9,25},{17,1},{25,9},{2,18},{10... | collective-permute-start | bytes 3080 | tf_op jit(solution)/shard_map/ppermute | solution.py:208
  34.0 0.0 collective-permute-start.10
  34.0 0.0 collective-permute-done.8.cross1
  34.0 0.0 collective-permute-done.9.core1
  34.0 0.9 %collective-permute-done.12.rest_3_ = f32[2,128]{1,0:T(2,128)S(1)} collective-permute-done((f32[2,128]{1,0:T(2,128)S(1)}, f32[2,128]{1,0:T(2,128)S(1)}, u32[]{:S(2)}, u32[]{:S(2)}) %collective-permute-start.12) | collective-permute-done | bytes 1056 | tf_op jit(solution)/shard_map/ppermute | solution.py:208
  34.9 2.3 %collective-permute-done.11.rest_2_ = f32[2,128]{1,0:T(2,128)S(1)} collective-permute-done((f32[2,128]{1,0:T(2,128)S(1)}, f32[2,128]{1,0:T(2,128)S(1)}, u32[]{:S(2)}, u32[]{:S(2)}) %collective-permute-start.11) | collective-permute-done | bytes 1056 | tf_op jit(solution)/shard_map/ppermute | solution.py:208
  37.2 0.0 collective-permute-done.10.rest_1_
  37.2 0.9 %shard_map.64 = (f32[2,2,2,128,128]{4,3,2,1,0:T(8,128)}, f32[2,128]{1,0:T(2,128)}) custom-call(f32[6,2,128,128]{3,2,1,0:T(8,128)S(1)} %get-tuple-element.43.total0, f32[6,2,128,128]{3,2,1,0:T(8,128)S(1)} %get-tuple-element.47.total1, f32[2,2,128,128]{3,2,1,0:T(8,128)S(1)} %collective-permute-done.6.cross0, ...), custom_call_target="tpu_custom_call" | custom-call | flops 1000000 | bytes 2000000 | tf_op jit(solution)/shard_map/pallas_call | solution.py:278
Async XLA Ops:
  2.2 10.2 %collective-permute-start = (f32[2,2,128,128]{3,2,1,0:T(8,128)S(1)}, f32[2,2,128,128]{3,2,1,0:T(8,128)S(1)}, u32[]{:S(2)}, u32[]{:S(2)}) collective-permute-start(f32[2,2,128,128]{3,2,1,0:T(8,128)S(1)} %get-tuple-element.32.green0), channel_id=1, source_target_pairs={{0,1},{2,3},{4,5},{6,7},{1,0},{3,2},{5,4},{7,6},{8,9},{10,11},{12,... | collective-permute-start | bytes 786440 | tf_op jit(solution)/shard_map/ppermute | solution.py:29
  5.2 14.2 %collective-permute-start.4 = (f32[2,2,2,128,128]{4,3,2,1,0:T(8,128)S(1)}, f32[2,2,2,128,128]{4,3,2,1,0:T(8,128)S(1)}, u32[]{:S(2)}, u32[]{:S(2)}) collective-permute-start(f32[2,2,2,128,128]{4,3,2,1,0:T(8,128)S(1)} %get-tuple-element.40.green), channel_id=1, source_target_pairs={{8,16},{0,24},{16,8},{24,0},{9,17},{1,25},{17,9},{25,1},{10,18},{2... | collective-permute-start | bytes 1572872 | tf_op jit(solution)/shard_map/ppermute | solution.py:29
  5.8 13.5 %collective-permute-start.3 = (f32[2,2,2,128,128]{4,3,2,1,0:T(8,128)S(1)}, f32[2,2,2,128,128]{4,3,2,1,0:T(8,128)S(1)}, u32[]{:S(2)}, u32[]{:S(2)}) collective-permute-start(f32[2,2,2,128,128]{4,3,2,1,0:T(8,128)S(1)} %get-tuple-element.40.green), channel_id=1, source_target_pairs={{0,8},{16,24},{8,0},{24,16},{1,9},{17,25},{9,1},{25,17},{2,10},{18... | collective-permute-start | bytes 1572872 | tf_op jit(solution)/shard_map/ppermute | solution.py:29
  6.8 10.3 %collective-permute-start.2 = (f32[2,2,128,128]{3,2,1,0:T(8,128)S(1)}, f32[2,2,128,128]{3,2,1,0:T(8,128)S(1)}, u32[]{:S(2)}, u32[]{:S(2)}) collective-permute-start(f32[2,2,128,128]{3,2,1,0:T(8,128)S(1)} %get-tuple-element.44.green1), channel_id=1, source_target_pairs={{0,1},{2,3},{4,5},{6,7},{1,0},{3,2},{5,4},{7,6},{8,9},{10,11},{12,... | collective-permute-start | bytes 786440 | tf_op jit(solution)/shard_map/ppermute | solution.py:29
  12.3 10.7 %collective-permute-start.1 = (f32[2,2,128,128]{3,2,1,0:T(8,128)S(1)}, f32[2,2,128,128]{3,2,1,0:T(8,128)S(1)}, u32[]{:S(2)}, u32[]{:S(2)}) collective-permute-start(f32[2,2,128,128]{3,2,1,0:T(8,128)S(1)} %collective-permute-done.ahead0), channel_id=1, source_target_pairs={{0,2},{2,4},{4,6},{3,1},{5,3},{7,5},{8,10},{10,12},{12,14},{11,9},... | collective-permute-start | bytes 786440 | tf_op jit(solution)/shard_map/ppermute | solution.py:36
  16.3 9.0 %collective-permute-start.5 = (f32[2,2,128,128]{3,2,1,0:T(8,128)S(1)}, f32[2,2,128,128]{3,2,1,0:T(8,128)S(1)}, u32[]{:S(2)}, u32[]{:S(2)}) collective-permute-start(f32[2,2,128,128]{3,2,1,0:T(8,128)S(1)} %get-tuple-element.44.green1), channel_id=1, source_target_pairs={{1,2},{3,4},{5,6},{2,1},{4,3},{6,5},{9,10},{11,12},{13,14},{10,9},... | collective-permute-start | bytes 786440 | tf_op jit(solution)/shard_map/ppermute | solution.py:29
  23.9 8.4 %collective-permute-start.6 = (f32[2,2,128,128]{3,2,1,0:T(8,128)S(1)}, f32[2,2,128,128]{3,2,1,0:T(8,128)S(1)}, u32[]{:S(2)}, u32[]{:S(2)}) collective-permute-start(f32[2,2,128,128]{3,2,1,0:T(8,128)S(1)} %get-tuple-element.48), channel_id=1, source_target_pairs={{8,16},{0,24},{16,8},{24,0},{9,17},{1,25},{17,9},{25,1},{10,18},{2... | collective-permute-start | bytes 786440 | tf_op jit(solution)/shard_map/ppermute | solution.py:29
  24.7 7.6 %collective-permute-start.7 = (f32[2,2,128,128]{3,2,1,0:T(8,128)S(1)}, f32[2,2,128,128]{3,2,1,0:T(8,128)S(1)}, u32[]{:S(2)}, u32[]{:S(2)}) collective-permute-start(f32[2,2,128,128]{3,2,1,0:T(8,128)S(1)} %get-tuple-element.49), channel_id=1, source_target_pairs={{0,8},{16,24},{8,0},{24,16},{1,9},{17,25},{9,1},{25,17},{2,10},{18... | collective-permute-start | bytes 786440 | tf_op jit(solution)/shard_map/ppermute | solution.py:29
  26.2 7.8 %collective-permute-start.8 = (f32[2,2,128,128]{3,2,1,0:T(8,128)S(1)}, f32[2,2,128,128]{3,2,1,0:T(8,128)S(1)}, u32[]{:S(2)}, u32[]{:S(2)}) collective-permute-start(f32[2,2,128,128]{3,2,1,0:T(8,128)S(1)} %get-tuple-element.53), channel_id=1, source_target_pairs={{8,16},{16,8},{9,17},{17,9},{10,18},{18,10},{11,19},{19,11},{12,20... | collective-permute-start | bytes 786440 | tf_op jit(solution)/shard_map/ppermute | solution.py:29
  26.9 7.1 %collective-permute-start.9 = (f32[2,2,128,128]{3,2,1,0:T(8,128)S(1)}, f32[2,2,128,128]{3,2,1,0:T(8,128)S(1)}, u32[]{:S(2)}, u32[]{:S(2)}) collective-permute-start(f32[2,2,128,128]{3,2,1,0:T(8,128)S(1)} %get-tuple-element.54), channel_id=1, source_target_pairs={{0,8},{16,24},{8,0},{24,16},{1,9},{17,25},{9,1},{25,17},{2,10},{18... | collective-permute-start | bytes 786440 | tf_op jit(solution)/shard_map/ppermute | solution.py:29
  32.3 2.6 %collective-permute-start.12 = (f32[2,128]{1,0:T(2,128)S(1)}, f32[2,128]{1,0:T(2,128)S(1)}, u32[]{:S(2)}, u32[]{:S(2)}) collective-permute-start(f32[2,128]{1,0:T(2,128)S(1)} %get-tuple-element.55.rest_0_), channel_id=1, source_target_pairs={{0,24},{8,0},{16,8},{24,16},{1,25},{9,1},{17,9},{25,17},{2,26},{10... | collective-permute-start | bytes 3080 | tf_op jit(solution)/shard_map/ppermute | solution.py:208
  33.6 3.6 %collective-permute-start.11 = (f32[2,128]{1,0:T(2,128)S(1)}, f32[2,128]{1,0:T(2,128)S(1)}, u32[]{:S(2)}, u32[]{:S(2)}) collective-permute-start(f32[2,128]{1,0:T(2,128)S(1)} %get-tuple-element.55.rest_0_), channel_id=1, source_target_pairs={{0,16},{8,24},{16,0},{24,8},{1,17},{9,25},{17,1},{25,9},{2,18},{10... | collective-permute-start | bytes 3080 | tf_op jit(solution)/shard_map/ppermute | solution.py:208
  34.0 3.1 %collective-permute-start.10 = (f32[2,128]{1,0:T(2,128)S(1)}, f32[2,128]{1,0:T(2,128)S(1)}, u32[]{:S(2)}, u32[]{:S(2)}) collective-permute-start(f32[2,128]{1,0:T(2,128)S(1)} %get-tuple-element.55.rest_0_), channel_id=1, source_target_pairs={{0,8},{8,16},{16,24},{24,0},{1,9},{9,17},{17,25},{25,1},{2,10},{10... | collective-permute-start | bytes 3080 | tf_op jit(solution)/shard_map/ppermute | solution.py:208
where the time goes:
time: 37.8 us; the launch traced here: 38.1 us
  starting transfers between devices  15.9 us (42%)
  waiting for transfers between devices  11.6 us (31%)
  Pallas kernels  9.82 us (26%)
  between operations  0.71 us (2%)
    ppermute x9, starting transfers between devices, swap(): return lax.ppermute(x, axis, pairs + [(j, i) for i, j in pairs])  10.1 us
    ppermute x9, waiting for transfers between devices, swap(): return lax.ppermute(x, axis, pairs + [(j, i) for i, j in pairs])  8.51 us
    pallas_call x4, Pallas kernels, call(): pl.pallas_call(kernel, out_shape=[jax.ShapeDtypeStruct(shape, jnp.float32...  7.4 us
    ppermute x1, starting transfers between devices, forward(): return lax.ppermute(x, axis, ups + downs)  4.02 us
    ppermute x3, waiting for transfers between devices, addends(): return [x] + [lax.ppermute(x, axis, turn) for turn in turns]  3.13 us
    ppermute x3, starting transfers between devices, addends(): return [x] + [lax.ppermute(x, axis, turn) for turn in turns]  1.76 us
    pallas_call x1, Pallas kernels, per_device(): pl.pallas_call(fetch_kernel, out_shape=[jax.ShapeDtypeStruct(green.shape[...  1.51 us
    pallas_call x1, Pallas kernels, per_device(): pl.pallas_call(functools.partial(end_kernel, energies), out_shape=[jax.Sh...  0.9 us
  transfers between devices with their start and end apart: 13, of which 6 were waited for; matrix products, arithmetic and copies ran while one was open for 0% of the time, Pallas kernels for 19%

commit v1 on v0

--- a/solution.py
+++ b/solution.py
@@ -272,9 +272,11 @@
         [spread, edge, edge, (a_local, orb)],
         (across1, total1, turned, partial),
     )
-    core1, cross1 = swap(core1, "energy", 0), swap(cross1, "energy", 1)
-    cross0, core0, rate = lax.optimization_barrier((cross0, core0, rate))
+    cross1 = swap(cross1, "energy", 1)
+    core0, rate = lax.optimization_barrier((core0, rate))
     rates = addends(rate, "energy")
+    cross0, core1, rates = lax.optimization_barrier((cross0, core1, rates))
+    core1 = swap(core1, "energy", 0)
     return pl.pallas_call(
         functools.partial(end_kernel, energies),
         out_shape=[

time: 37.8 us -> 37.6 us (level)
  the two profiles are of different devices: /device:TPU:0 before, /device:TPU:17 now
where the time goes in v1:
time: 37.6 us
  starting transfers between devices  15.3 us (41%)
  waiting for transfers between devices  11.1 us (30%)
  Pallas kernels  10.5 us (28%)
  between operations  0.71 us (2%)
    ppermute x9, waiting for transfers between devices, swap(): return lax.ppermute(x, axis, pairs + [(j, i) for i, j in pairs])  11 us
    ppermute x9, starting transfers between devices, swap(): return lax.ppermute(x, axis, pairs + [(j, i) for i, j in pairs])  9.44 us
    pallas_call x4, Pallas kernels, call(): pl.pallas_call(kernel, out_shape=[jax.ShapeDtypeStruct(shape, jnp.float32...  8.1 us
    ppermute x1, starting transfers between devices, forward(): return lax.ppermute(x, axis, ups + downs)  3.19 us
    ppermute x3, starting transfers between devices, addends(): return [x] + [lax.ppermute(x, axis, turn) for turn in turns]  2.63 us
    pallas_call x1, Pallas kernels, per_device(): pl.pallas_call(fetch_kernel, out_shape=[jax.ShapeDtypeStruct(green.shape[...  1.51 us
    pallas_call x1, Pallas kernels, per_device(): pl.pallas_call(functools.partial(end_kernel, energies), out_shape=[jax.Sh...  0.92 us
  transfers between devices with their start and end apart: 13, of which 5 were waited for; matrix products, arithmetic and copies ran while one was open for 0% of the time, Pallas kernels for 22%

profile of v1, /device:TPU:17, one launch (start us, length us, event | category | flops | bytes accessed | tf_op | source)
XLA Modules:
  0.0 37.6 jit_solution(911845240337093332)
XLA Ops:
  0.6 1.5 %shard_map.59 = (f32[2,2,128,128]{3,2,1,0:T(8,128)S(1)}, f32[2,2,128,128]{3,2,1,0:T(8,128)S(1)}, f32[2,2,2,128,128]{4,3,2,1,0:T(8,128)S(1)}, f32[2,6,128,128]{3,...) custom-call(f32[2,2,2,128,128]{4,3,2,1,0:T(8,128)} %green.1, f32[2,6,128,128]{3,2,1,0:T(8,128)} %coupling.1, ...), custom_call_target="tpu_custom_call" | custom-call | tf_op jit(solution)/shard_map/pallas_call | solution.py:243
  2.2 1.3 %collective-permute-start = (f32[2,2,128,128]{3,2,1,0:T(8,128)S(1)}, f32[2,2,128,128]{3,2,1,0:T(8,128)S(1)}, u32[]{:S(2)}, u32[]{:S(2)}) collective-permute-start(f32[2,2,128,128]{3,2,1,0:T(8,128)S(1)} %get-tuple-element.37.green0), channel_id=1, source_target_pairs={{0,1},{2,3},{4,5},{6,7},{1,0},{3,2},{5,4},{7,6},{8,9},{10,11},{12,... | collective-permute-start | bytes 786440 | tf_op jit(solution)/shard_map/ppermute | solution.py:29
  3.5 2.1 %collective-permute-start.4 = (f32[2,2,2,128,128]{4,3,2,1,0:T(8,128)S(1)}, f32[2,2,2,128,128]{4,3,2,1,0:T(8,128)S(1)}, u32[]{:S(2)}, u32[]{:S(2)}) collective-permute-start(f32[2,2,2,128,128]{4,3,2,1,0:T(8,128)S(1)} %get-tuple-element.45.green), channel_id=1, source_target_pairs={{8,16},{0,24},{16,8},{24,0},{9,17},{1,25},{17,9},{25,1},{10,18},{2... | collective-permute-start | bytes 1572872 | tf_op jit(solution)/shard_map/ppermute | solution.py:29
  5.5 0.0 collective-permute-start.3
  5.5 0.2 collective-permute-start.2
  5.7 1.4 %shard_map.60 = (f32[6,2,128,128]{3,2,1,0:T(8,128)S(1)}, f32[6,2,128,128]{3,2,1,0:T(8,128)S(1)}) custom-call(s32[2,6]{1,0:T(2,128)S(1)} %get-tuple-element.34.neighbours, f32[2,4,6]{2,1,0:T(4,128)S(1)} %get-tuple-element.35.phonon, f32[2,6,128,128]{3,2,1,0:T(8,128)S(1)} %get-tuple-element.36.coupling, f32[2,2,128,128]{3,2,1,0:T(8,128)S(1)} %get-tuple-element.37.green0, ...), custom_call_target="tpu_custom_call" | custom-call | flops 1000000 | bytes 10000 | tf_op jit(solution)/shard_map/pallas_call | solution.py:229
  7.2 2.2 %collective-permute-done.ahead0 = f32[2,2,128,128]{3,2,1,0:T(8,128)S(1)} collective-permute-done((f32[2,2,128,128]{3,2,1,0:T(8,128)S(1)}, f32[2,2,128,128]{3,2,1,0:T(8,128)S(1)}, u32[]{:S(2)}, u32[]{:S(2)}) %collective-permute-start) | collective-permute-done | bytes 262176 | tf_op jit(solution)/shard_map/ppermute | solution.py:29
  9.4 3.2 %collective-permute-start.1 = (f32[2,2,128,128]{3,2,1,0:T(8,128)S(1)}, f32[2,2,128,128]{3,2,1,0:T(8,128)S(1)}, u32[]{:S(2)}, u32[]{:S(2)}) collective-permute-start(f32[2,2,128,128]{3,2,1,0:T(8,128)S(1)} %collective-permute-done.ahead0), channel_id=1, source_target_pairs={{0,2},{2,4},{4,6},{3,1},{5,3},{7,5},{8,10},{10,12},{12,14},{11,9},... | collective-permute-start | bytes 786440 | tf_op jit(solution)/shard_map/ppermute | solution.py:36
  12.6 1.9 %collective-permute-start.5 = (f32[2,2,128,128]{3,2,1,0:T(8,128)S(1)}, f32[2,2,128,128]{3,2,1,0:T(8,128)S(1)}, u32[]{:S(2)}, u32[]{:S(2)}) collective-permute-start(f32[2,2,128,128]{3,2,1,0:T(8,128)S(1)} %get-tuple-element.49.green1), channel_id=1, source_target_pairs={{1,2},{3,4},{5,6},{2,1},{4,3},{6,5},{9,10},{11,12},{13,14},{10,9},... | collective-permute-start | bytes 786440 | tf_op jit(solution)/shard_map/ppermute | solution.py:29
  14.5 0.5 %collective-permute-done.2.ahead1 = f32[2,2,128,128]{3,2,1,0:T(8,128)S(1)} collective-permute-done((f32[2,2,128,128]{3,2,1,0:T(8,128)S(1)}, f32[2,2,128,128]{3,2,1,0:T(8,128)S(1)}, u32[]{:S(2)}, u32[]{:S(2)}) %collective-permute-start.2) | collective-permute-done | bytes 262176 | tf_op jit(solution)/shard_map/ppermute | solution.py:29
  15.0 3.2 %collective-permute-done.4.by_cross = f32[2,2,2,128,128]{4,3,2,1,0:T(8,128)S(1)} collective-permute-done((f32[2,2,2,128,128]{4,3,2,1,0:T(8,128)S(1)}, f32[2,2,2,128,128]{4,3,2,1,0:T(8,128)S(1)}, u32[]{:S(2)}, u32[]{:S(2)}) %collective-permute-start.4) | collective-permute-done | bytes 524320 | tf_op jit(solution)/shard_map/ppermute | solution.py:29
  18.2 0.0 collective-permute-done.3.by_core
  18.2 2.4 %shard_map.61 = (f32[6,2,128,128]{3,2,1,0:T(8,128)S(1)}, f32[6,2,128,128]{3,2,1,0:T(8,128)S(1)}, f32[2,6,2,128,128]{4,3,2,1,0:T(8,128)S(1)}) custom-call(s32[2,6]{1,0:T(2,128)S(1)} %get-tuple-element.34.neighbours, f32[2,4,6]{2,1,0:T(4,128)S(1)} %get-tuple-element.35.phonon, f32[2,6,128,128]{3,2,1,0:T(8,128)S(1)} %get-tuple-element.36.coupling, ...), custom_call_target="tpu_custom_call" | custom-call | flops 1000000 | bytes 10000 | tf_op jit(solution)/shard_map/pallas_call | solution.py:229
  20.7 0.0 collective-permute-done.1.across
  20.7 2.1 %shard_map.62 = (f32[6,2,128,128]{3,2,1,0:T(8,128)S(1)}, f32[2,2,128,128]{3,2,1,0:T(8,128)S(1)}, f32[2,2,128,128]{3,2,1,0:T(8,128)S(1)}, f32[2,128,128]{2,1,0:T(8,128)S(1)}) custom-call(s32[2,6]{1,0:T(2,128)S(1)} %get-tuple-element.34.neighbours, f32[2,4,6]{2,1,0:T(4,128)S(1)} %get-tuple-element.35.phonon, ...), custom_call_target="tpu_custom_call" | custom-call | flops 1000000 | bytes 10000 | tf_op jit(solution)/shard_map/pallas_call | solution.py:229
  22.8 0.4 %collective-permute-start.7 = (f32[2,2,128,128]{3,2,1,0:T(8,128)S(1)}, f32[2,2,128,128]{3,2,1,0:T(8,128)S(1)}, u32[]{:S(2)}, u32[]{:S(2)}) collective-permute-start(f32[2,2,128,128]{3,2,1,0:T(8,128)S(1)} %get-tuple-element.55), channel_id=1, source_target_pairs={{0,8},{16,24},{8,0},{24,16},{1,9},{17,25},{9,1},{25,17},{2,10},{18... | collective-permute-start | bytes 786440 | tf_op jit(solution)/shard_map/ppermute | solution.py:29
  23.2 1.0 %collective-permute-start.6 = (f32[2,2,128,128]{3,2,1,0:T(8,128)S(1)}, f32[2,2,128,128]{3,2,1,0:T(8,128)S(1)}, u32[]{:S(2)}, u32[]{:S(2)}) collective-permute-start(f32[2,2,128,128]{3,2,1,0:T(8,128)S(1)} %get-tuple-element.53), channel_id=1, source_target_pairs={{8,16},{0,24},{16,8},{24,0},{9,17},{1,25},{17,9},{25,1},{10,18},{2... | collective-permute-start | bytes 786440 | tf_op jit(solution)/shard_map/ppermute | solution.py:29
  24.2 0.0 collective-permute-done.5.across
  24.2 2.1 %shard_map.63 = (f32[6,2,128,128]{3,2,1,0:T(8,128)S(1)}, f32[2,2,128,128]{3,2,1,0:T(8,128)S(1)}, f32[2,2,128,128]{3,2,1,0:T(8,128)S(1)}, f32[2,128]{1,0:T(2,128)S(1)}) custom-call(s32[2,6]{1,0:T(2,128)S(1)} %get-tuple-element.34.neighbours, f32[2,4,6]{2,1,0:T(4,128)S(1)} %get-tuple-element.35.phonon, f32[2,6,128,128]{3,2,1,0:T(8,128)S(1)} %get-tuple-element.36.coupling, ...), custom_call_target="tpu_custom_call" | custom-call | flops 1000000 | bytes 10000 | tf_op jit(solution)/shard_map/pallas_call | solution.py:229
  26.3 0.0 collective-permute-done.7.core0
  26.3 0.6 %collective-permute-start.10 = (f32[2,128]{1,0:T(2,128)S(1)}, f32[2,128]{1,0:T(2,128)S(1)}, u32[]{:S(2)}, u32[]{:S(2)}) collective-permute-start(f32[2,128]{1,0:T(2,128)S(1)} %get-tuple-element.62.rest_0_), channel_id=1, source_target_pairs={{0,24},{8,0},{16,8},{24,16},{1,25},{9,1},{17,9},{25,17},{2,26},{10... | collective-permute-start | bytes 3080 | tf_op jit(solution)/shard_map/ppermute | solution.py:208
  26.9 1.2 %collective-permute-start.9 = (f32[2,128]{1,0:T(2,128)S(1)}, f32[2,128]{1,0:T(2,128)S(1)}, u32[]{:S(2)}, u32[]{:S(2)}) collective-permute-start(f32[2,128]{1,0:T(2,128)S(1)} %get-tuple-element.62.rest_0_), channel_id=1, source_target_pairs={{0,16},{8,24},{16,0},{24,8},{1,17},{9,25},{17,1},{25,9},{2,18},{10... | collective-permute-start | bytes 3080 | tf_op jit(solution)/shard_map/ppermute | solution.py:208
  28.2 0.8 %collective-permute-start.8 = (f32[2,128]{1,0:T(2,128)S(1)}, f32[2,128]{1,0:T(2,128)S(1)}, u32[]{:S(2)}, u32[]{:S(2)}) collective-permute-start(f32[2,128]{1,0:T(2,128)S(1)} %get-tuple-element.62.rest_0_), channel_id=1, source_target_pairs={{0,8},{8,16},{16,24},{24,0},{1,9},{9,17},{17,25},{25,1},{2,10},{10... | collective-permute-start | bytes 3080 | tf_op jit(solution)/shard_map/ppermute | solution.py:208
  29.0 1.9 %collective-permute-start.11 = (f32[2,2,128,128]{3,2,1,0:T(8,128)S(1)}, f32[2,2,128,128]{3,2,1,0:T(8,128)S(1)}, u32[]{:S(2)}, u32[]{:S(2)}) collective-permute-start(f32[2,2,128,128]{3,2,1,0:T(8,128)S(1)} %get-tuple-element.60), channel_id=1, source_target_pairs={{8,16},{16,8},{9,17},{17,9},{10,18},{18,10},{11,19},{19,11},{12,20... | collective-permute-start | bytes 786440 | tf_op jit(solution)/shard_map/ppermute | solution.py:29
  30.9 0.4 %collective-permute-done.6.cross0 = f32[2,2,128,128]{3,2,1,0:T(8,128)S(1)} collective-permute-done((f32[2,2,128,128]{3,2,1,0:T(8,128)S(1)}, f32[2,2,128,128]{3,2,1,0:T(8,128)S(1)}, u32[]{:S(2)}, u32[]{:S(2)}) %collective-permute-start.6) | collective-permute-done | bytes 262176 | tf_op jit(solution)/shard_map/ppermute | solution.py:29
  31.3 0.0 collective-permute-done.10.rest_3_
  31.4 0.0 collective-permute-done.9.rest_2_
  31.4 0.0 collective-permute-done.8.rest_1_
  31.4 0.7 %collective-permute-start.12 = (f32[2,2,128,128]{3,2,1,0:T(8,128)S(1)}, f32[2,2,128,128]{3,2,1,0:T(8,128)S(1)}, u32[]{:S(2)}, u32[]{:S(2)}) collective-permute-start(f32[2,2,128,128]{3,2,1,0:T(8,128)S(1)} %get-tuple-element.61), channel_id=1, source_target_pairs={{0,8},{16,24},{8,0},{24,16},{1,9},{17,25},{9,1},{25,17},{2,10},{18... | collective-permute-start | bytes 786440 | tf_op jit(solution)/shard_map/ppermute | solution.py:29
  32.0 4.6 %collective-permute-done.11.cross1 = f32[2,2,128,128]{3,2,1,0:T(8,128)S(1)} collective-permute-done((f32[2,2,128,128]{3,2,1,0:T(8,128)S(1)}, f32[2,2,128,128]{3,2,1,0:T(8,128)S(1)}, u32[]{:S(2)}, u32[]{:S(2)}) %collective-permute-start.11) | collective-permute-done | bytes 262176 | tf_op jit(solution)/shard_map/ppermute | solution.py:29
  36.6 0.0 collective-permute-done.12.core1
  36.7 0.9 %shard_map.64 = (f32[2,2,2,128,128]{4,3,2,1,0:T(8,128)}, f32[2,128]{1,0:T(2,128)}) custom-call(f32[6,2,128,128]{3,2,1,0:T(8,128)S(1)} %get-tuple-element.48.total0, f32[6,2,128,128]{3,2,1,0:T(8,128)S(1)} %get-tuple-element.52.total1, f32[2,2,128,128]{3,2,1,0:T(8,128)S(1)} %collective-permute-done.6.cross0, ...), custom_call_target="tpu_custom_call" | custom-call | flops 1000000 | bytes 2000000 | tf_op jit(solution)/shard_map/pallas_call | solution.py:280
Async XLA Ops:
  2.2 7.2 %collective-permute-start = (f32[2,2,128,128]{3,2,1,0:T(8,128)S(1)}, f32[2,2,128,128]{3,2,1,0:T(8,128)S(1)}, u32[]{:S(2)}, u32[]{:S(2)}) collective-permute-start(f32[2,2,128,128]{3,2,1,0:T(8,128)S(1)} %get-tuple-element.37.green0), channel_id=1, source_target_pairs={{0,1},{2,3},{4,5},{6,7},{1,0},{3,2},{5,4},{7,6},{8,9},{10,11},{12,... | collective-permute-start | bytes 786440 | tf_op jit(solution)/shard_map/ppermute | solution.py:29
  3.5 14.8 %collective-permute-start.4 = (f32[2,2,2,128,128]{4,3,2,1,0:T(8,128)S(1)}, f32[2,2,2,128,128]{4,3,2,1,0:T(8,128)S(1)}, u32[]{:S(2)}, u32[]{:S(2)}) collective-permute-start(f32[2,2,2,128,128]{4,3,2,1,0:T(8,128)S(1)} %get-tuple-element.45.green), channel_id=1, source_target_pairs={{8,16},{0,24},{16,8},{24,0},{9,17},{1,25},{17,9},{25,1},{10,18},{2... | collective-permute-start | bytes 1572872 | tf_op jit(solution)/shard_map/ppermute | solution.py:29
  5.5 12.7 %collective-permute-start.3 = (f32[2,2,2,128,128]{4,3,2,1,0:T(8,128)S(1)}, f32[2,2,2,128,128]{4,3,2,1,0:T(8,128)S(1)}, u32[]{:S(2)}, u32[]{:S(2)}) collective-permute-start(f32[2,2,2,128,128]{4,3,2,1,0:T(8,128)S(1)} %get-tuple-element.45.green), channel_id=1, source_target_pairs={{0,8},{16,24},{8,0},{24,16},{1,9},{17,25},{9,1},{25,17},{2,10},{18... | collective-permute-start | bytes 1572872 | tf_op jit(solution)/shard_map/ppermute | solution.py:29
  5.5 9.5 %collective-permute-start.2 = (f32[2,2,128,128]{3,2,1,0:T(8,128)S(1)}, f32[2,2,128,128]{3,2,1,0:T(8,128)S(1)}, u32[]{:S(2)}, u32[]{:S(2)}) collective-permute-start(f32[2,2,128,128]{3,2,1,0:T(8,128)S(1)} %get-tuple-element.49.green1), channel_id=1, source_target_pairs={{0,1},{2,3},{4,5},{6,7},{1,0},{3,2},{5,4},{7,6},{8,9},{10,11},{12,... | collective-permute-start | bytes 786440 | tf_op jit(solution)/shard_map/ppermute | solution.py:29
  9.4 11.3 %collective-permute-start.1 = (f32[2,2,128,128]{3,2,1,0:T(8,128)S(1)}, f32[2,2,128,128]{3,2,1,0:T(8,128)S(1)}, u32[]{:S(2)}, u32[]{:S(2)}) collective-permute-start(f32[2,2,128,128]{3,2,1,0:T(8,128)S(1)} %collective-permute-done.ahead0), channel_id=1, source_target_pairs={{0,2},{2,4},{4,6},{3,1},{5,3},{7,5},{8,10},{10,12},{12,14},{11,9},... | collective-permute-start | bytes 786440 | tf_op jit(solution)/shard_map/ppermute | solution.py:36
  12.6 11.6 %collective-permute-start.5 = (f32[2,2,128,128]{3,2,1,0:T(8,128)S(1)}, f32[2,2,128,128]{3,2,1,0:T(8,128)S(1)}, u32[]{:S(2)}, u32[]{:S(2)}) collective-permute-start(f32[2,2,128,128]{3,2,1,0:T(8,128)S(1)} %get-tuple-element.49.green1), channel_id=1, source_target_pairs={{1,2},{3,4},{5,6},{2,1},{4,3},{6,5},{9,10},{11,12},{13,14},{10,9},... | collective-permute-start | bytes 786440 | tf_op jit(solution)/shard_map/ppermute | solution.py:29
  22.8 3.5 %collective-permute-start.7 = (f32[2,2,128,128]{3,2,1,0:T(8,128)S(1)}, f32[2,2,128,128]{3,2,1,0:T(8,128)S(1)}, u32[]{:S(2)}, u32[]{:S(2)}) collective-permute-start(f32[2,2,128,128]{3,2,1,0:T(8,128)S(1)} %get-tuple-element.55), channel_id=1, source_target_pairs={{0,8},{16,24},{8,0},{24,16},{1,9},{17,25},{9,1},{25,17},{2,10},{18... | collective-permute-start | bytes 786440 | tf_op jit(solution)/shard_map/ppermute | solution.py:29
  23.2 8.1 %collective-permute-start.6 = (f32[2,2,128,128]{3,2,1,0:T(8,128)S(1)}, f32[2,2,128,128]{3,2,1,0:T(8,128)S(1)}, u32[]{:S(2)}, u32[]{:S(2)}) collective-permute-start(f32[2,2,128,128]{3,2,1,0:T(8,128)S(1)} %get-tuple-element.53), channel_id=1, source_target_pairs={{8,16},{0,24},{16,8},{24,0},{9,17},{1,25},{17,9},{25,1},{10,18},{2... | collective-permute-start | bytes 786440 | tf_op jit(solution)/shard_map/ppermute | solution.py:29
  26.3 5.0 %collective-permute-start.10 = (f32[2,128]{1,0:T(2,128)S(1)}, f32[2,128]{1,0:T(2,128)S(1)}, u32[]{:S(2)}, u32[]{:S(2)}) collective-permute-start(f32[2,128]{1,0:T(2,128)S(1)} %get-tuple-element.62.rest_0_), channel_id=1, source_target_pairs={{0,24},{8,0},{16,8},{24,16},{1,25},{9,1},{17,9},{25,17},{2,26},{10... | collective-permute-start | bytes 3080 | tf_op jit(solution)/shard_map/ppermute | solution.py:208
  26.9 4.4 %collective-permute-start.9 = (f32[2,128]{1,0:T(2,128)S(1)}, f32[2,128]{1,0:T(2,128)S(1)}, u32[]{:S(2)}, u32[]{:S(2)}) collective-permute-start(f32[2,128]{1,0:T(2,128)S(1)} %get-tuple-element.62.rest_0_), channel_id=1, source_target_pairs={{0,16},{8,24},{16,0},{24,8},{1,17},{9,25},{17,1},{25,9},{2,18},{10... | collective-permute-start | bytes 3080 | tf_op jit(solution)/shard_map/ppermute | solution.py:208
  28.2 3.2 %collective-permute-start.8 = (f32[2,128]{1,0:T(2,128)S(1)}, f32[2,128]{1,0:T(2,128)S(1)}, u32[]{:S(2)}, u32[]{:S(2)}) collective-permute-start(f32[2,128]{1,0:T(2,128)S(1)} %get-tuple-element.62.rest_0_), channel_id=1, source_target_pairs={{0,8},{8,16},{16,24},{24,0},{1,9},{9,17},{17,25},{25,1},{2,10},{10... | collective-permute-start | bytes 3080 | tf_op jit(solution)/shard_map/ppermute | solution.py:208
  29.0 7.7 %collective-permute-start.11 = (f32[2,2,128,128]{3,2,1,0:T(8,128)S(1)}, f32[2,2,128,128]{3,2,1,0:T(8,128)S(1)}, u32[]{:S(2)}, u32[]{:S(2)}) collective-permute-start(f32[2,2,128,128]{3,2,1,0:T(8,128)S(1)} %get-tuple-element.60), channel_id=1, source_target_pairs={{8,16},{16,8},{9,17},{17,9},{10,18},{18,10},{11,19},{19,11},{12,20... | collective-permute-start | bytes 786440 | tf_op jit(solution)/shard_map/ppermute | solution.py:29
  31.4 5.3 %collective-permute-start.12 = (f32[2,2,128,128]{3,2,1,0:T(8,128)S(1)}, f32[2,2,128,128]{3,2,1,0:T(8,128)S(1)}, u32[]{:S(2)}, u32[]{:S(2)}) collective-permute-start(f32[2,2,128,128]{3,2,1,0:T(8,128)S(1)} %get-tuple-element.61), channel_id=1, source_target_pairs={{0,8},{16,24},{8,0},{24,16},{1,9},{17,25},{9,1},{25,17},{2,10},{18... | collective-permute-start | bytes 786440 | tf_op jit(solution)/shard_map/ppermute | solution.py:29

commit v2 on v0

--- a/solution.py
+++ b/solution.py
@@ -256,7 +256,7 @@
     ahead0, total0, total1 = lax.optimization_barrier((ahead0, total0, total1))
     across0 = forward(ahead0, "atom")
     green1, ahead0 = lax.optimization_barrier((green1, ahead0))
-    across1 = swap(green1, "atom", 1)
+    across1 = swap(green1, "atom", 1, close=True)
     total0, total1, turned = call(
         functools.partial(pair_kernel, energies),
         [spread, spread, (2,) + spread],

time: 37.8 us -> 41.5 us (1.098)
  the two profiles are of different devices: /device:TPU:0 before, /device:TPU:16 now
where the time goes in v2:
time: 41.5 us; the launch traced here: 41.6 us
  waiting for transfers between devices  16.9 us (41%)
  starting transfers between devices  13.6 us (33%)
  Pallas kernels  10.5 us (25%)
  between operations  0.71 us (2%)
    ppermute x9, waiting for transfers between devices, swap(): return lax.ppermute(x, axis, pairs + [(j, i) for i, j in pairs])  11 us
    ppermute x9, starting transfers between devices, swap(): return lax.ppermute(x, axis, pairs + [(j, i) for i, j in pairs])  8.33 us
    pallas_call x4, Pallas kernels, call(): pl.pallas_call(kernel, out_shape=[jax.ShapeDtypeStruct(shape, jnp.float32...  8.05 us
    ppermute x1, starting transfers between devices, forward(): return lax.ppermute(x, axis, ups + downs)  3.47 us
    ppermute x3, waiting for transfers between devices, addends(): return [x] + [lax.ppermute(x, axis, turn) for turn in turns]  2.97 us
    ppermute x1, waiting for transfers between devices, forward(): return lax.ppermute(x, axis, ups + downs)  2.86 us
    ppermute x3, starting transfers between devices, addends(): return [x] + [lax.ppermute(x, axis, turn) for turn in turns]  1.75 us
    pallas_call x1, Pallas kernels, per_device(): pl.pallas_call(fetch_kernel, out_shape=[jax.ShapeDtypeStruct(green.shape[...  1.51 us
  transfers between devices with their start and end apart: 13, of which 6 were waited for; matrix products, arithmetic and copies ran while one was open for 0% of the time, Pallas kernels for 19%

profile of v2, /device:TPU:16, one launch (start us, length us, event | category | flops | bytes accessed | tf_op | source)
XLA Modules:
  0.0 41.6 jit_solution(15355377328655192502)
XLA Ops:
  0.6 1.5 %shard_map.59 = (f32[2,2,128,128]{3,2,1,0:T(8,128)S(1)}, f32[2,2,128,128]{3,2,1,0:T(8,128)S(1)}, f32[2,2,2,128,128]{4,3,2,1,0:T(8,128)S(1)}, f32[2,6,128,128]{3,...) custom-call(f32[2,2,2,128,128]{4,3,2,1,0:T(8,128)} %green.1, f32[2,6,128,128]{3,2,1,0:T(8,128)} %coupling.1, ...), custom_call_target="tpu_custom_call" | custom-call | tf_op jit(solution)/shard_map/pallas_call | solution.py:243
  2.2 1.6 %collective-permute-start = (f32[2,2,128,128]{3,2,1,0:T(8,128)S(1)}, f32[2,2,128,128]{3,2,1,0:T(8,128)S(1)}, u32[]{:S(2)}, u32[]{:S(2)}) collective-permute-start(f32[2,2,128,128]{3,2,1,0:T(8,128)S(1)} %get-tuple-element.32.green0), channel_id=1, source_target_pairs={{0,1},{2,3},{4,5},{6,7},{1,0},{3,2},{5,4},{7,6},{8,9},{10,11},{12,... | collective-permute-start | bytes 786440 | tf_op jit(solution)/shard_map/ppermute | solution.py:29
  3.7 0.7 %collective-permute-start.4 = (f32[2,2,2,128,128]{4,3,2,1,0:T(8,128)S(1)}, f32[2,2,2,128,128]{4,3,2,1,0:T(8,128)S(1)}, u32[]{:S(2)}, u32[]{:S(2)}) collective-permute-start(f32[2,2,2,128,128]{4,3,2,1,0:T(8,128)S(1)} %get-tuple-element.40.green), channel_id=1, source_target_pairs={{8,16},{0,24},{16,8},{24,0},{9,17},{1,25},{17,9},{25,1},{10,18},{2... | collective-permute-start | bytes 1572872 | tf_op jit(solution)/shard_map/ppermute | solution.py:29
  4.4 1.0 %collective-permute-start.3 = (f32[2,2,2,128,128]{4,3,2,1,0:T(8,128)S(1)}, f32[2,2,2,128,128]{4,3,2,1,0:T(8,128)S(1)}, u32[]{:S(2)}, u32[]{:S(2)}) collective-permute-start(f32[2,2,2,128,128]{4,3,2,1,0:T(8,128)S(1)} %get-tuple-element.40.green), channel_id=1, source_target_pairs={{0,8},{16,24},{8,0},{24,16},{1,9},{17,25},{9,1},{25,17},{2,10},{18... | collective-permute-start | bytes 1572872 | tf_op jit(solution)/shard_map/ppermute | solution.py:29
  5.3 0.5 %collective-permute-start.2 = (f32[2,2,128,128]{3,2,1,0:T(8,128)S(1)}, f32[2,2,128,128]{3,2,1,0:T(8,128)S(1)}, u32[]{:S(2)}, u32[]{:S(2)}) collective-permute-start(f32[2,2,128,128]{3,2,1,0:T(8,128)S(1)} %get-tuple-element.44.green1), channel_id=1, source_target_pairs={{0,1},{2,3},{4,5},{6,7},{1,0},{3,2},{5,4},{7,6},{8,9},{10,11},{12,... | collective-permute-start | bytes 786440 | tf_op jit(solution)/shard_map/ppermute | solution.py:29
  5.9 2.0 %shard_map.60 = (f32[6,2,128,128]{3,2,1,0:T(8,128)S(1)}, f32[6,2,128,128]{3,2,1,0:T(8,128)S(1)}) custom-call(s32[2,6]{1,0:T(2,128)S(1)} %get-tuple-element.29.neighbours, f32[2,4,6]{2,1,0:T(4,128)S(1)} %get-tuple-element.30.phonon, f32[2,6,128,128]{3,2,1,0:T(8,128)S(1)} %get-tuple-element.31.coupling, f32[2,2,128,128]{3,2,1,0:T(8,128)S(1)} %get-tuple-element.32.green0, ...), custom_call_target="tpu_custom_call" | custom-call | flops 1000000 | bytes 10000 | tf_op jit(solution)/shard_map/pallas_call | solution.py:229
  7.9 3.5 %collective-permute-done.ahead0 = f32[2,2,128,128]{3,2,1,0:T(8,128)S(1)} collective-permute-done((f32[2,2,128,128]{3,2,1,0:T(8,128)S(1)}, f32[2,2,128,128]{3,2,1,0:T(8,128)S(1)}, u32[]{:S(2)}, u32[]{:S(2)}) %collective-permute-start) | collective-permute-done | bytes 262176 | tf_op jit(solution)/shard_map/ppermute | solution.py:29
  11.4 3.5 %collective-permute-start.1 = (f32[2,2,128,128]{3,2,1,0:T(8,128)S(1)}, f32[2,2,128,128]{3,2,1,0:T(8,128)S(1)}, u32[]{:S(2)}, u32[]{:S(2)}) collective-permute-start(f32[2,2,128,128]{3,2,1,0:T(8,128)S(1)} %collective-permute-done.ahead0), channel_id=1, source_target_pairs={{0,2},{2,4},{4,6},{3,1},{5,3},{7,5},{8,10},{10,12},{12,14},{11,9},... | collective-permute-start | bytes 786440 | tf_op jit(solution)/shard_map/ppermute | solution.py:36
  14.9 0.3 collective-permute-start.5
  15.2 5.3 %collective-permute-done.2.ahead1 = f32[2,2,128,128]{3,2,1,0:T(8,128)S(1)} collective-permute-done((f32[2,2,128,128]{3,2,1,0:T(8,128)S(1)}, f32[2,2,128,128]{3,2,1,0:T(8,128)S(1)}, u32[]{:S(2)}, u32[]{:S(2)}) %collective-permute-start.2) | collective-permute-done | bytes 262176 | tf_op jit(solution)/shard_map/ppermute | solution.py:29
  20.6 0.0 collective-permute-done.4.by_cross
  20.6 0.0 collective-permute-done.3.by_core
  20.6 1.8 %shard_map.61 = (f32[6,2,128,128]{3,2,1,0:T(8,128)S(1)}, f32[6,2,128,128]{3,2,1,0:T(8,128)S(1)}, f32[2,6,2,128,128]{4,3,2,1,0:T(8,128)S(1)}) custom-call(s32[2,6]{1,0:T(2,128)S(1)} %get-tuple-element.29.neighbours, f32[2,4,6]{2,1,0:T(4,128)S(1)} %get-tuple-element.30.phonon, f32[2,6,128,128]{3,2,1,0:T(8,128)S(1)} %get-tuple-element.31.coupling, ...), custom_call_target="tpu_custom_call" | custom-call | flops 1000000 | bytes 10000 | tf_op jit(solution)/shard_map/pallas_call | solution.py:229
  22.4 2.9 %collective-permute-done.1.across = f32[2,2,128,128]{3,2,1,0:T(8,128)S(1)} collective-permute-done((f32[2,2,128,128]{3,2,1,0:T(8,128)S(1)}, f32[2,2,128,128]{3,2,1,0:T(8,128)S(1)}, u32[]{:S(2)}, u32[]{:S(2)}) %collective-permute-start.1) | collective-permute-done | bytes 262176 | tf_op jit(solution)/shard_map/ppermute | solution.py:36
  25.3 2.1 %shard_map.62 = (f32[6,2,128,128]{3,2,1,0:T(8,128)S(1)}, f32[2,2,128,128]{3,2,1,0:T(8,128)S(1)}, f32[2,2,128,128]{3,2,1,0:T(8,128)S(1)}, f32[2,128,128]{2,1,0:T(8,128)S(1)}) custom-call(s32[2,6]{1,0:T(2,128)S(1)} %get-tuple-element.29.neighbours, f32[2,4,6]{2,1,0:T(4,128)S(1)} %get-tuple-element.30.phonon, ...), custom_call_target="tpu_custom_call" | custom-call | flops 1000000 | bytes 10000 | tf_op jit(solution)/shard_map/pallas_call | solution.py:229
  27.3 0.1 collective-permute-start.6
  27.4 1.6 %collective-permute-start.7 = (f32[2,2,128,128]{3,2,1,0:T(8,128)S(1)}, f32[2,2,128,128]{3,2,1,0:T(8,128)S(1)}, u32[]{:S(2)}, u32[]{:S(2)}) collective-permute-start(f32[2,2,128,128]{3,2,1,0:T(8,128)S(1)} %get-tuple-element.49), channel_id=1, source_target_pairs={{0,8},{16,24},{8,0},{24,16},{1,9},{17,25},{9,1},{25,17},{2,10},{18... | collective-permute-start | bytes 786440 | tf_op jit(solution)/shard_map/ppermute | solution.py:29
  29.0 0.0 collective-permute-done.5.across
  29.0 2.1 %shard_map.63 = (f32[6,2,128,128]{3,2,1,0:T(8,128)S(1)}, f32[2,2,128,128]{3,2,1,0:T(8,128)S(1)}, f32[2,2,128,128]{3,2,1,0:T(8,128)S(1)}, f32[2,128]{1,0:T(2,128)S(1)}) custom-call(s32[2,6]{1,0:T(2,128)S(1)} %get-tuple-element.29.neighbours, f32[2,4,6]{2,1,0:T(4,128)S(1)} %get-tuple-element.30.phonon, f32[2,6,128,128]{3,2,1,0:T(8,128)S(1)} %get-tuple-element.31.coupling, ...), custom_call_target="tpu_custom_call" | custom-call | flops 1000000 | bytes 10000 | tf_op jit(solution)/shard_map/pallas_call | solution.py:229
  31.2 0.7 %collective-permute-start.8 = (f32[2,2,128,128]{3,2,1,0:T(8,128)S(1)}, f32[2,2,128,128]{3,2,1,0:T(8,128)S(1)}, u32[]{:S(2)}, u32[]{:S(2)}) collective-permute-start(f32[2,2,128,128]{3,2,1,0:T(8,128)S(1)} %get-tuple-element.53), channel_id=1, source_target_pairs={{8,16},{16,8},{9,17},{17,9},{10,18},{18,10},{11,19},{19,11},{12,20... | collective-permute-start | bytes 786440 | tf_op jit(solution)/shard_map/ppermute | solution.py:29
  31.9 1.9 %collective-permute-start.9 = (f32[2,2,128,128]{3,2,1,0:T(8,128)S(1)}, f32[2,2,128,128]{3,2,1,0:T(8,128)S(1)}, u32[]{:S(2)}, u32[]{:S(2)}) collective-permute-start(f32[2,2,128,128]{3,2,1,0:T(8,128)S(1)} %get-tuple-element.54), channel_id=1, source_target_pairs={{0,8},{16,24},{8,0},{24,16},{1,9},{17,25},{9,1},{25,17},{2,10},{18... | collective-permute-start | bytes 786440 | tf_op jit(solution)/shard_map/ppermute | solution.py:29
  33.8 2.2 %collective-permute-done.6.cross0 = f32[2,2,128,128]{3,2,1,0:T(8,128)S(1)} collective-permute-done((f32[2,2,128,128]{3,2,1,0:T(8,128)S(1)}, f32[2,2,128,128]{3,2,1,0:T(8,128)S(1)}, u32[]{:S(2)}, u32[]{:S(2)}) %collective-permute-start.6) | collective-permute-done | bytes 262176 | tf_op jit(solution)/shard_map/ppermute | solution.py:29
  36.0 0.0 collective-permute-done.7.core0
  36.0 0.0 collective-permute-start.12
  36.0 1.7 %collective-permute-start.11 = (f32[2,128]{1,0:T(2,128)S(1)}, f32[2,128]{1,0:T(2,128)S(1)}, u32[]{:S(2)}, u32[]{:S(2)}) collective-permute-start(f32[2,128]{1,0:T(2,128)S(1)} %get-tuple-element.55.rest_0_), channel_id=1, source_target_pairs={{0,16},{8,24},{16,0},{24,8},{1,17},{9,25},{17,1},{25,9},{2,18},{10... | collective-permute-start | bytes 3080 | tf_op jit(solution)/shard_map/ppermute | solution.py:208
  37.7 0.0 collective-permute-start.10
  37.7 0.0 collective-permute-done.8.cross1
  37.7 0.0 collective-permute-done.9.core1
  37.7 0.0 collective-permute-done.12.rest_3_
  37.7 1.8 %collective-permute-done.11.rest_2_ = f32[2,128]{1,0:T(2,128)S(1)} collective-permute-done((f32[2,128]{1,0:T(2,128)S(1)}, f32[2,128]{1,0:T(2,128)S(1)}, u32[]{:S(2)}, u32[]{:S(2)}) %collective-permute-start.11) | collective-permute-done | bytes 1056 | tf_op jit(solution)/shard_map/ppermute | solution.py:208
  39.5 1.2 %collective-permute-done.10.rest_1_ = f32[2,128]{1,0:T(2,128)S(1)} collective-permute-done((f32[2,128]{1,0:T(2,128)S(1)}, f32[2,128]{1,0:T(2,128)S(1)}, u32[]{:S(2)}, u32[]{:S(2)}) %collective-permute-start.10) | collective-permute-done | bytes 1056 | tf_op jit(solution)/shard_map/ppermute | solution.py:208
  40.7 0.9 %shard_map.64 = (f32[2,2,2,128,128]{4,3,2,1,0:T(8,128)}, f32[2,128]{1,0:T(2,128)}) custom-call(f32[6,2,128,128]{3,2,1,0:T(8,128)S(1)} %get-tuple-element.43.total0, f32[6,2,128,128]{3,2,1,0:T(8,128)S(1)} %get-tuple-element.47.total1, f32[2,2,128,128]{3,2,1,0:T(8,128)S(1)} %collective-permute-done.6.cross0, ...), custom_call_target="tpu_custom_call" | custom-call | flops 1000000 | bytes 2000000 | tf_op jit(solution)/shard_map/pallas_call | solution.py:278
Async XLA Ops:
  2.2 9.3 %collective-permute-start = (f32[2,2,128,128]{3,2,1,0:T(8,128)S(1)}, f32[2,2,128,128]{3,2,1,0:T(8,128)S(1)}, u32[]{:S(2)}, u32[]{:S(2)}) collective-permute-start(f32[2,2,128,128]{3,2,1,0:T(8,128)S(1)} %get-tuple-element.32.green0), channel_id=1, source_target_pairs={{0,1},{2,3},{4,5},{6,7},{1,0},{3,2},{5,4},{7,6},{8,9},{10,11},{12,... | collective-permute-start | bytes 786440 | tf_op jit(solution)/shard_map/ppermute | solution.py:29
  3.7 16.8 %collective-permute-start.4 = (f32[2,2,2,128,128]{4,3,2,1,0:T(8,128)S(1)}, f32[2,2,2,128,128]{4,3,2,1,0:T(8,128)S(1)}, u32[]{:S(2)}, u32[]{:S(2)}) collective-permute-start(f32[2,2,2,128,128]{4,3,2,1,0:T(8,128)S(1)} %get-tuple-element.40.green), channel_id=1, source_target_pairs={{8,16},{0,24},{16,8},{24,0},{9,17},{1,25},{17,9},{25,1},{10,18},{2... | collective-permute-start | bytes 1572872 | tf_op jit(solution)/shard_map/ppermute | solution.py:29
  4.4 16.2 %collective-permute-start.3 = (f32[2,2,2,128,128]{4,3,2,1,0:T(8,128)S(1)}, f32[2,2,2,128,128]{4,3,2,1,0:T(8,128)S(1)}, u32[]{:S(2)}, u32[]{:S(2)}) collective-permute-start(f32[2,2,2,128,128]{4,3,2,1,0:T(8,128)S(1)} %get-tuple-element.40.green), channel_id=1, source_target_pairs={{0,8},{16,24},{8,0},{24,16},{1,9},{17,25},{9,1},{25,17},{2,10},{18... | collective-permute-start | bytes 1572872 | tf_op jit(solution)/shard_map/ppermute | solution.py:29
  5.3 15.2 %collective-permute-start.2 = (f32[2,2,128,128]{3,2,1,0:T(8,128)S(1)}, f32[2,2,128,128]{3,2,1,0:T(8,128)S(1)}, u32[]{:S(2)}, u32[]{:S(2)}) collective-permute-start(f32[2,2,128,128]{3,2,1,0:T(8,128)S(1)} %get-tuple-element.44.green1), channel_id=1, source_target_pairs={{0,1},{2,3},{4,5},{6,7},{1,0},{3,2},{5,4},{7,6},{8,9},{10,11},{12,... | collective-permute-start | bytes 786440 | tf_op jit(solution)/shard_map/ppermute | solution.py:29
  11.4 13.9 %collective-permute-start.1 = (f32[2,2,128,128]{3,2,1,0:T(8,128)S(1)}, f32[2,2,128,128]{3,2,1,0:T(8,128)S(1)}, u32[]{:S(2)}, u32[]{:S(2)}) collective-permute-start(f32[2,2,128,128]{3,2,1,0:T(8,128)S(1)} %collective-permute-done.ahead0), channel_id=1, source_target_pairs={{0,2},{2,4},{4,6},{3,1},{5,3},{7,5},{8,10},{10,12},{12,14},{11,9},... | collective-permute-start | bytes 786440 | tf_op jit(solution)/shard_map/ppermute | solution.py:36
  14.9 14.1 %collective-permute-start.5 = (f32[2,2,128,128]{3,2,1,0:T(8,128)S(1)}, f32[2,2,128,128]{3,2,1,0:T(8,128)S(1)}, u32[]{:S(2)}, u32[]{:S(2)}) collective-permute-start(f32[2,2,128,128]{3,2,1,0:T(8,128)S(1)} %get-tuple-element.44.green1), channel_id=1, source_target_pairs={{1,2},{3,4},{5,6},{0,7},{2,1},{4,3},{6,5},{7,0},{9,10},{11,12},{13... | collective-permute-start | bytes 786440 | tf_op jit(solution)/shard_map/ppermute | solution.py:29
  27.3 8.6 %collective-permute-start.6 = (f32[2,2,128,128]{3,2,1,0:T(8,128)S(1)}, f32[2,2,128,128]{3,2,1,0:T(8,128)S(1)}, u32[]{:S(2)}, u32[]{:S(2)}) collective-permute-start(f32[2,2,128,128]{3,2,1,0:T(8,128)S(1)} %get-tuple-element.48), channel_id=1, source_target_pairs={{8,16},{0,24},{16,8},{24,0},{9,17},{1,25},{17,9},{25,1},{10,18},{2... | collective-permute-start | bytes 786440 | tf_op jit(solution)/shard_map/ppermute | solution.py:29
  27.4 8.5 %collective-permute-start.7 = (f32[2,2,128,128]{3,2,1,0:T(8,128)S(1)}, f32[2,2,128,128]{3,2,1,0:T(8,128)S(1)}, u32[]{:S(2)}, u32[]{:S(2)}) collective-permute-start(f32[2,2,128,128]{3,2,1,0:T(8,128)S(1)} %get-tuple-element.49), channel_id=1, source_target_pairs={{0,8},{16,24},{8,0},{24,16},{1,9},{17,25},{9,1},{25,17},{2,10},{18... | collective-permute-start | bytes 786440 | tf_op jit(solution)/shard_map/ppermute | solution.py:29
  31.2 6.5 %collective-permute-start.8 = (f32[2,2,128,128]{3,2,1,0:T(8,128)S(1)}, f32[2,2,128,128]{3,2,1,0:T(8,128)S(1)}, u32[]{:S(2)}, u32[]{:S(2)}) collective-permute-start(f32[2,2,128,128]{3,2,1,0:T(8,128)S(1)} %get-tuple-element.53), channel_id=1, source_target_pairs={{8,16},{16,8},{9,17},{17,9},{10,18},{18,10},{11,19},{19,11},{12,20... | collective-permute-start | bytes 786440 | tf_op jit(solution)/shard_map/ppermute | solution.py:29
  31.9 5.9 %collective-permute-start.9 = (f32[2,2,128,128]{3,2,1,0:T(8,128)S(1)}, f32[2,2,128,128]{3,2,1,0:T(8,128)S(1)}, u32[]{:S(2)}, u32[]{:S(2)}) collective-permute-start(f32[2,2,128,128]{3,2,1,0:T(8,128)S(1)} %get-tuple-element.54), channel_id=1, source_target_pairs={{0,8},{16,24},{8,0},{24,16},{1,9},{17,25},{9,1},{25,17},{2,10},{18... | collective-permute-start | bytes 786440 | tf_op jit(solution)/shard_map/ppermute | solution.py:29
  36.0 1.8 %collective-permute-start.12 = (f32[2,128]{1,0:T(2,128)S(1)}, f32[2,128]{1,0:T(2,128)S(1)}, u32[]{:S(2)}, u32[]{:S(2)}) collective-permute-start(f32[2,128]{1,0:T(2,128)S(1)} %get-tuple-element.55.rest_0_), channel_id=1, source_target_pairs={{0,24},{8,0},{16,8},{24,16},{1,25},{9,1},{17,9},{25,17},{2,26},{10... | collective-permute-start | bytes 3080 | tf_op jit(solution)/shard_map/ppermute | solution.py:208
  36.0 3.6 %collective-permute-start.11 = (f32[2,128]{1,0:T(2,128)S(1)}, f32[2,128]{1,0:T(2,128)S(1)}, u32[]{:S(2)}, u32[]{:S(2)}) collective-permute-start(f32[2,128]{1,0:T(2,128)S(1)} %get-tuple-element.55.rest_0_), channel_id=1, source_target_pairs={{0,16},{8,24},{16,0},{24,8},{1,17},{9,25},{17,1},{25,9},{2,18},{10... | collective-permute-start | bytes 3080 | tf_op jit(solution)/shard_map/ppermute | solution.py:208
  37.7 3.0 %collective-permute-start.10 = (f32[2,128]{1,0:T(2,128)S(1)}, f32[2,128]{1,0:T(2,128)S(1)}, u32[]{:S(2)}, u32[]{:S(2)}) collective-permute-start(f32[2,128]{1,0:T(2,128)S(1)} %get-tuple-element.55.rest_0_), channel_id=1, source_target_pairs={{0,8},{8,16},{16,24},{24,0},{1,9},{9,17},{17,25},{25,1},{2,10},{10... | collective-permute-start | bytes 3080 | tf_op jit(solution)/shard_map/ppermute | solution.py:208

commit v3 on v0

--- a/solution.py
+++ b/solution.py
@@ -29,11 +29,25 @@
     return lax.ppermute(x, axis, pairs + [(j, i) for i, j in pairs])
 
 
+def cross_swap(x):
+    energies, atoms = lax.axis_size("energy"), lax.axis_size("atom")
+    perm = []
+    for e in range(energies):
+        other = e + 1 if e % 2 else e - 1
+        for a in range(atoms):
+            if 0 <= other < energies:
+                perm.append((e * atoms + a, other * atoms + a))
+            elif atoms % 2 == 0:
+                perm.append((e * atoms + a, e * atoms + (a ^ 1)))
+    return lax.ppermute(x, ("energy", "atom"), perm)
+
+
 def forward(x, axis):
     size = lax.axis_size(axis)
-    ups = [(i, i + 2) for i in range(0, size - 2, 2)]
-    downs = [(i + 2, i) for i in range(1, size - 2, 2)]
-    return lax.ppermute(x, axis, ups + downs)
+    steps = [(i, i + 2 if i % 2 == 0 else i - 2) for i in range(size)]
+    if size % 2 == 0 and size > 2:
+        return lax.ppermute(x, axis, [(i, j % size) for i, j in steps])
+    return lax.ppermute(x, axis, [(i, j) for i, j in steps if 0 <= j < size])
 
 
 def put_blocks(blocks, c, green):
@@ -266,13 +280,13 @@
     total0, core0, cross0, partial = call(
         far_kernel, [spread, edge, edge, (a_local, orb, orb)], (across0, total0, turned)
     )
-    core0, cross0 = swap(core0, "energy", 0), swap(cross0, "energy", 1, close=True)
+    core0, cross0 = swap(core0, "energy", 0), cross_swap(cross0)
     total1, core1, cross1, rate = call(
         functools.partial(last_kernel, 1.0 / (4.0 * points)),
         [spread, edge, edge, (a_local, orb)],
         (across1, total1, turned, partial),
     )
-    core1, cross1 = swap(core1, "energy", 0), swap(cross1, "energy", 1)
+    core1, cross1 = swap(core1, "energy", 0), cross_swap(cross1)
     cross0, core0, rate = lax.optimization_barrier((cross0, core0, rate))
     rates = addends(rate, "energy")
     return pl.pallas_call(

time: 37.8 us -> 36.5 us (0.966)
  starting transfers between devices: 15.9 us -> 14.4 us
  waiting for transfers between devices: 11.6 us -> 10.9 us
  Pallas kernels: 9.82 us -> 10.4 us
    ppermute x1 -> x3, waiting for transfers between devices: 0.01 us -> 5.37 us  [the longest x2 2.83 us: cross_swap(): return lax.ppermute(x, ('energy', 'atom'), perm)]
    ppermute x9 -> x7, starting transfers between devices: 10.1 us -> 5.85 us  [swap(): return lax.ppermute(x, axis, pairs + [(j, i) for i, j in pairs])]
    ppermute x9 -> x7, waiting for transfers between devices: 8.51 us -> 4.78 us  [swap(): return lax.ppermute(x, axis, pairs + [(j, i) for i, j in pairs])]
    ppermute x1 -> x3, starting transfers between devices: 4.02 us -> 7 us  [the longest x2 4.89 us: cross_swap(): return lax.ppermute(x, ('energy', 'atom'), perm)]
    ppermute x3, waiting for transfers between devices: 3.13 us -> 0.78 us  [addends(): return [x] + [lax.ppermute(x, axis, turn) for turn in turns]]
    pallas_call x4, Pallas kernels: 7.4 us -> 8.03 us  [call(): pl.pallas_call(kernel, out_shape=[jax.ShapeDtypeStruct(shape, jnp.float32...]
  transfers between devices with their start and end apart: 13 -> 13, of which waited for: 6 -> 7; matrix products, arithmetic and copies ran while one was open for 0% -> 0% of each run, Pallas kernels for 19% -> 22%
where the time goes in v3:
time: 36.5 us; the launch traced here: 36.4 us
  starting transfers between devices  14.4 us (39%)
  waiting for transfers between devices  10.9 us (30%)
  Pallas kernels  10.4 us (28%)
  between operations  0.68 us (2%)
    pallas_call x4, Pallas kernels, call(): pl.pallas_call(kernel, out_shape=[jax.ShapeDtypeStruct(shape, jnp.float32...  8.03 us
    ppermute x7, starting transfers between devices, swap(): return lax.ppermute(x, axis, pairs + [(j, i) for i, j in pairs])  5.85 us
    ppermute x2, starting transfers between devices, cross_swap(): return lax.ppermute(x, ('energy', 'atom'), perm)  4.89 us
    ppermute x7, waiting for transfers between devices, swap(): return lax.ppermute(x, axis, pairs + [(j, i) for i, j in pairs])  4.78 us
    ppermute x2, waiting for transfers between devices, cross_swap(): return lax.ppermute(x, ('energy', 'atom'), perm)  2.83 us
    ppermute x1, waiting for transfers between devices, forward(): return lax.ppermute(x, axis, [(i, j % size) for i, j in steps])  2.54 us
    ppermute x1, starting transfers between devices, forward(): return lax.ppermute(x, axis, [(i, j % size) for i, j in steps])  2.12 us
    pallas_call x1, Pallas kernels, per_device(): pl.pallas_call(fetch_kernel, out_shape=[jax.ShapeDtypeStruct(green.shape[...  1.51 us
  transfers between devices with their start and end apart: 13, of which 7 were waited for; matrix products, arithmetic and copies ran while one was open for 0% of the time, Pallas kernels for 22%

profile of v3, /device:TPU:0, one launch (start us, length us, event | category | flops | bytes accessed | tf_op | source)
XLA Modules:
  0.0 36.4 jit_solution(5647057686410585043)
XLA Ops:
  0.6 1.5 %shard_map.59 = (f32[2,2,128,128]{3,2,1,0:T(8,128)S(1)}, f32[2,2,128,128]{3,2,1,0:T(8,128)S(1)}, f32[2,2,2,128,128]{4,3,2,1,0:T(8,128)S(1)}, f32[2,6,128,128]{3,...) custom-call(f32[2,2,2,128,128]{4,3,2,1,0:T(8,128)} %green.1, f32[2,6,128,128]{3,2,1,0:T(8,128)} %coupling.1, ...), custom_call_target="tpu_custom_call" | custom-call | tf_op jit(solution)/shard_map/pallas_call | solution.py:257
  2.2 3.0 %collective-permute-start = (f32[2,2,128,128]{3,2,1,0:T(8,128)S(1)}, f32[2,2,128,128]{3,2,1,0:T(8,128)S(1)}, u32[]{:S(2)}, u32[]{:S(2)}) collective-permute-start(f32[2,2,128,128]{3,2,1,0:T(8,128)S(1)} %get-tuple-element.32.green0), channel_id=1, source_target_pairs={{0,1},{2,3},{4,5},{6,7},{1,0},{3,2},{5,4},{7,6},{8,9},{10,11},{12,... | collective-permute-start | bytes 786440 | tf_op jit(solution)/shard_map/ppermute | solution.py:29
  5.2 0.7 %collective-permute-start.4 = (f32[2,2,2,128,128]{4,3,2,1,0:T(8,128)S(1)}, f32[2,2,2,128,128]{4,3,2,1,0:T(8,128)S(1)}, u32[]{:S(2)}, u32[]{:S(2)}) collective-permute-start(f32[2,2,2,128,128]{4,3,2,1,0:T(8,128)S(1)} %get-tuple-element.40.green), channel_id=1, source_target_pairs={{8,16},{0,24},{16,8},{24,0},{9,17},{1,25},{17,9},{25,1},{10,18},{2... | collective-permute-start | bytes 1572872 | tf_op jit(solution)/shard_map/ppermute | solution.py:29
  5.8 1.0 %collective-permute-start.3 = (f32[2,2,2,128,128]{4,3,2,1,0:T(8,128)S(1)}, f32[2,2,2,128,128]{4,3,2,1,0:T(8,128)S(1)}, u32[]{:S(2)}, u32[]{:S(2)}) collective-permute-start(f32[2,2,2,128,128]{4,3,2,1,0:T(8,128)S(1)} %get-tuple-element.40.green), channel_id=1, source_target_pairs={{0,8},{16,24},{8,0},{24,16},{1,9},{17,25},{9,1},{25,17},{2,10},{18... | collective-permute-start | bytes 1572872 | tf_op jit(solution)/shard_map/ppermute | solution.py:29
  6.8 0.5 %collective-permute-start.2 = (f32[2,2,128,128]{3,2,1,0:T(8,128)S(1)}, f32[2,2,128,128]{3,2,1,0:T(8,128)S(1)}, u32[]{:S(2)}, u32[]{:S(2)}) collective-permute-start(f32[2,2,128,128]{3,2,1,0:T(8,128)S(1)} %get-tuple-element.44.green1), channel_id=1, source_target_pairs={{0,1},{2,3},{4,5},{6,7},{1,0},{3,2},{5,4},{7,6},{8,9},{10,11},{12,... | collective-permute-start | bytes 786440 | tf_op jit(solution)/shard_map/ppermute | solution.py:29
  7.3 4.5 %shard_map.60 = (f32[6,2,128,128]{3,2,1,0:T(8,128)S(1)}, f32[6,2,128,128]{3,2,1,0:T(8,128)S(1)}) custom-call(s32[2,6]{1,0:T(2,128)S(1)} %get-tuple-element.29.neighbours, f32[2,4,6]{2,1,0:T(4,128)S(1)} %get-tuple-element.30.phonon, f32[2,6,128,128]{3,2,1,0:T(8,128)S(1)} %get-tuple-element.31.coupling, f32[2,2,128,128]{3,2,1,0:T(8,128)S(1)} %get-tuple-element.32.green0, ...), custom_call_target="tpu_custom_call" | custom-call | flops 1000000 | bytes 10000 | tf_op jit(solution)/shard_map/pallas_call | solution.py:243
  11.8 0.5 %collective-permute-done.ahead0 = f32[2,2,128,128]{3,2,1,0:T(8,128)S(1)} collective-permute-done((f32[2,2,128,128]{3,2,1,0:T(8,128)S(1)}, f32[2,2,128,128]{3,2,1,0:T(8,128)S(1)}, u32[]{:S(2)}, u32[]{:S(2)}) %collective-permute-start) | collective-permute-done | bytes 262176 | tf_op jit(solution)/shard_map/ppermute | solution.py:29
  12.3 2.1 %collective-permute-start.1 = (f32[2,2,128,128]{3,2,1,0:T(8,128)S(1)}, f32[2,2,128,128]{3,2,1,0:T(8,128)S(1)}, u32[]{:S(2)}, u32[]{:S(2)}) collective-permute-start(f32[2,2,128,128]{3,2,1,0:T(8,128)S(1)} %collective-permute-done.ahead0), channel_id=1, source_target_pairs={{0,2},{1,7},{2,4},{3,1},{4,6},{5,3},{6,0},{7,5},{8,10},{9,15},{10,... | collective-permute-start | bytes 786440 | tf_op jit(solution)/shard_map/ppermute | solution.py:49
  14.4 0.7 %collective-permute-start.5 = (f32[2,2,128,128]{3,2,1,0:T(8,128)S(1)}, f32[2,2,128,128]{3,2,1,0:T(8,128)S(1)}, u32[]{:S(2)}, u32[]{:S(2)}) collective-permute-start(f32[2,2,128,128]{3,2,1,0:T(8,128)S(1)} %get-tuple-element.44.green1), channel_id=1, source_target_pairs={{1,2},{3,4},{5,6},{2,1},{4,3},{6,5},{9,10},{11,12},{13,14},{10,9},... | collective-permute-start | bytes 786440 | tf_op jit(solution)/shard_map/ppermute | solution.py:29
  15.1 2.0 %collective-permute-done.2.ahead1 = f32[2,2,128,128]{3,2,1,0:T(8,128)S(1)} collective-permute-done((f32[2,2,128,128]{3,2,1,0:T(8,128)S(1)}, f32[2,2,128,128]{3,2,1,0:T(8,128)S(1)}, u32[]{:S(2)}, u32[]{:S(2)}) %collective-permute-start.2) | collective-permute-done | bytes 262176 | tf_op jit(solution)/shard_map/ppermute | solution.py:29
  17.1 2.3 %collective-permute-done.4.by_cross = f32[2,2,2,128,128]{4,3,2,1,0:T(8,128)S(1)} collective-permute-done((f32[2,2,2,128,128]{4,3,2,1,0:T(8,128)S(1)}, f32[2,2,2,128,128]{4,3,2,1,0:T(8,128)S(1)}, u32[]{:S(2)}, u32[]{:S(2)}) %collective-permute-start.4) | collective-permute-done | bytes 524320 | tf_op jit(solution)/shard_map/ppermute | solution.py:29
  19.4 0.0 collective-permute-done.3.by_core
  19.4 1.8 %shard_map.61 = (f32[6,2,128,128]{3,2,1,0:T(8,128)S(1)}, f32[6,2,128,128]{3,2,1,0:T(8,128)S(1)}, f32[2,6,2,128,128]{4,3,2,1,0:T(8,128)S(1)}) custom-call(s32[2,6]{1,0:T(2,128)S(1)} %get-tuple-element.29.neighbours, f32[2,4,6]{2,1,0:T(4,128)S(1)} %get-tuple-element.30.phonon, f32[2,6,128,128]{3,2,1,0:T(8,128)S(1)} %get-tuple-element.31.coupling, ...), custom_call_target="tpu_custom_call" | custom-call | flops 1000000 | bytes 10000 | tf_op jit(solution)/shard_map/pallas_call | solution.py:243
  21.2 2.5 %collective-permute-done.1.across = f32[2,2,128,128]{3,2,1,0:T(8,128)S(1)} collective-permute-done((f32[2,2,128,128]{3,2,1,0:T(8,128)S(1)}, f32[2,2,128,128]{3,2,1,0:T(8,128)S(1)}, u32[]{:S(2)}, u32[]{:S(2)}) %collective-permute-start.1) | collective-permute-done | bytes 262176 | tf_op jit(solution)/shard_map/ppermute | solution.py:49
  23.7 0.9 %shard_map.62 = (f32[6,2,128,128]{3,2,1,0:T(8,128)S(1)}, f32[2,2,128,128]{3,2,1,0:T(8,128)S(1)}, f32[2,2,128,128]{3,2,1,0:T(8,128)S(1)}, f32[2,128,128]{2,1,0:T(8,128)S(1)}) custom-call(s32[2,6]{1,0:T(2,128)S(1)} %get-tuple-element.29.neighbours, f32[2,4,6]{2,1,0:T(4,128)S(1)} %get-tuple-element.30.phonon, ...), custom_call_target="tpu_custom_call" | custom-call | flops 1000000 | bytes 10000 | tf_op jit(solution)/shard_map/pallas_call | solution.py:243
  24.6 1.7 %collective-permute-start.6 = (f32[2,2,128,128]{3,2,1,0:T(8,128)S(1)}, f32[2,2,128,128]{3,2,1,0:T(8,128)S(1)}, u32[]{:S(2)}, u32[]{:S(2)}) collective-permute-start(f32[2,2,128,128]{3,2,1,0:T(8,128)S(1)} %get-tuple-element.48), channel_id=1, source_target_pairs={{0,1},{1,0},{2,3},{3,2},{4,5},{5,4},{6,7},{7,6},{8,16},{9,17},{10,... | collective-permute-start | bytes 786440 | tf_op jit(solution)/shard_map/ppermute | solution.py:42
  26.2 0.0 collective-permute-start.7
  26.3 0.0 collective-permute-done.5.across
  26.3 0.9 %shard_map.63 = (f32[6,2,128,128]{3,2,1,0:T(8,128)S(1)}, f32[2,2,128,128]{3,2,1,0:T(8,128)S(1)}, f32[2,2,128,128]{3,2,1,0:T(8,128)S(1)}, f32[2,128]{1,0:T(2,128)S(1)}) custom-call(s32[2,6]{1,0:T(2,128)S(1)} %get-tuple-element.29.neighbours, f32[2,4,6]{2,1,0:T(4,128)S(1)} %get-tuple-element.30.phonon, f32[2,6,128,128]{3,2,1,0:T(8,128)S(1)} %get-tuple-element.31.coupling, ...), custom_call_target="tpu_custom_call" | custom-call | flops 1000000 | bytes 10000 | tf_op jit(solution)/shard_map/pallas_call | solution.py:243
  27.2 3.2 %collective-permute-start.8 = (f32[2,2,128,128]{3,2,1,0:T(8,128)S(1)}, f32[2,2,128,128]{3,2,1,0:T(8,128)S(1)}, u32[]{:S(2)}, u32[]{:S(2)}) collective-permute-start(f32[2,2,128,128]{3,2,1,0:T(8,128)S(1)} %get-tuple-element.53), channel_id=1, source_target_pairs={{0,1},{1,0},{2,3},{3,2},{4,5},{5,4},{6,7},{7,6},{8,16},{9,17},{10,... | collective-permute-start | bytes 786440 | tf_op jit(solution)/shard_map/ppermute | solution.py:42
  30.4 0.0 collective-permute-start.9
  30.4 0.6 %collective-permute-done.6.cross0 = f32[2,2,128,128]{3,2,1,0:T(8,128)S(1)} collective-permute-done((f32[2,2,128,128]{3,2,1,0:T(8,128)S(1)}, f32[2,2,128,128]{3,2,1,0:T(8,128)S(1)}, u32[]{:S(2)}, u32[]{:S(2)}) %collective-permute-start.6) | collective-permute-done | bytes 262176 | tf_op jit(solution)/shard_map/ppermute | solution.py:42
  31.0 0.0 collective-permute-done.7.core0
  31.0 0.0 collective-permute-start.12
  31.0 1.5 %collective-permute-start.11 = (f32[2,128]{1,0:T(2,128)S(1)}, f32[2,128]{1,0:T(2,128)S(1)}, u32[]{:S(2)}, u32[]{:S(2)}) collective-permute-start(f32[2,128]{1,0:T(2,128)S(1)} %get-tuple-element.55.rest_0_), channel_id=1, source_target_pairs={{0,16},{8,24},{16,0},{24,8},{1,17},{9,25},{17,1},{25,9},{2,18},{10... | collective-permute-start | bytes 3080 | tf_op jit(solution)/shard_map/ppermute | solution.py:222
  32.5 0.0 collective-permute-start.10
  32.5 2.2 %collective-permute-done.8.cross1 = f32[2,2,128,128]{3,2,1,0:T(8,128)S(1)} collective-permute-done((f32[2,2,128,128]{3,2,1,0:T(8,128)S(1)}, f32[2,2,128,128]{3,2,1,0:T(8,128)S(1)}, u32[]{:S(2)}, u32[]{:S(2)}) %collective-permute-start.8) | collective-permute-done | bytes 262176 | tf_op jit(solution)/shard_map/ppermute | solution.py:42
  34.7 0.0 collective-permute-done.9.core1
  34.7 0.0 collective-permute-done.12.rest_3_
  34.7 0.0 collective-permute-done.11.rest_2_
  34.7 0.8 %collective-permute-done.10.rest_1_ = f32[2,128]{1,0:T(2,128)S(1)} collective-permute-done((f32[2,128]{1,0:T(2,128)S(1)}, f32[2,128]{1,0:T(2,128)S(1)}, u32[]{:S(2)}, u32[]{:S(2)}) %collective-permute-start.10) | collective-permute-done | bytes 1056 | tf_op jit(solution)/shard_map/ppermute | solution.py:222
  35.5 0.9 %shard_map.64 = (f32[2,2,2,128,128]{4,3,2,1,0:T(8,128)}, f32[2,128]{1,0:T(2,128)}) custom-call(f32[6,2,128,128]{3,2,1,0:T(8,128)S(1)} %get-tuple-element.43.total0, f32[6,2,128,128]{3,2,1,0:T(8,128)S(1)} %get-tuple-element.47.total1, f32[2,2,128,128]{3,2,1,0:T(8,128)S(1)} %collective-permute-done.6.cross0, ...), custom_call_target="tpu_custom_call" | custom-call | flops 1000000 | bytes 2000000 | tf_op jit(solution)/shard_map/pallas_call | solution.py:292
Async XLA Ops:
  2.2 10.2 %collective-permute-start = (f32[2,2,128,128]{3,2,1,0:T(8,128)S(1)}, f32[2,2,128,128]{3,2,1,0:T(8,128)S(1)}, u32[]{:S(2)}, u32[]{:S(2)}) collective-permute-start(f32[2,2,128,128]{3,2,1,0:T(8,128)S(1)} %get-tuple-element.32.green0), channel_id=1, source_target_pairs={{0,1},{2,3},{4,5},{6,7},{1,0},{3,2},{5,4},{7,6},{8,9},{10,11},{12,... | collective-permute-start | bytes 786440 | tf_op jit(solution)/shard_map/ppermute | solution.py:29
  5.2 14.2 %collective-permute-start.4 = (f32[2,2,2,128,128]{4,3,2,1,0:T(8,128)S(1)}, f32[2,2,2,128,128]{4,3,2,1,0:T(8,128)S(1)}, u32[]{:S(2)}, u32[]{:S(2)}) collective-permute-start(f32[2,2,2,128,128]{4,3,2,1,0:T(8,128)S(1)} %get-tuple-element.40.green), channel_id=1, source_target_pairs={{8,16},{0,24},{16,8},{24,0},{9,17},{1,25},{17,9},{25,1},{10,18},{2... | collective-permute-start | bytes 1572872 | tf_op jit(solution)/shard_map/ppermute | solution.py:29
  5.8 13.5 %collective-permute-start.3 = (f32[2,2,2,128,128]{4,3,2,1,0:T(8,128)S(1)}, f32[2,2,2,128,128]{4,3,2,1,0:T(8,128)S(1)}, u32[]{:S(2)}, u32[]{:S(2)}) collective-permute-start(f32[2,2,2,128,128]{4,3,2,1,0:T(8,128)S(1)} %get-tuple-element.40.green), channel_id=1, source_target_pairs={{0,8},{16,24},{8,0},{24,16},{1,9},{17,25},{9,1},{25,17},{2,10},{18... | collective-permute-start | bytes 1572872 | tf_op jit(solution)/shard_map/ppermute | solution.py:29
  6.8 10.3 %collective-permute-start.2 = (f32[2,2,128,128]{3,2,1,0:T(8,128)S(1)}, f32[2,2,128,128]{3,2,1,0:T(8,128)S(1)}, u32[]{:S(2)}, u32[]{:S(2)}) collective-permute-start(f32[2,2,128,128]{3,2,1,0:T(8,128)S(1)} %get-tuple-element.44.green1), channel_id=1, source_target_pairs={{0,1},{2,3},{4,5},{6,7},{1,0},{3,2},{5,4},{7,6},{8,9},{10,11},{12,... | collective-permute-start | bytes 786440 | tf_op jit(solution)/shard_map/ppermute | solution.py:29
  12.3 11.4 %collective-permute-start.1 = (f32[2,2,128,128]{3,2,1,0:T(8,128)S(1)}, f32[2,2,128,128]{3,2,1,0:T(8,128)S(1)}, u32[]{:S(2)}, u32[]{:S(2)}) collective-permute-start(f32[2,2,128,128]{3,2,1,0:T(8,128)S(1)} %collective-permute-done.ahead0), channel_id=1, source_target_pairs={{0,2},{1,7},{2,4},{3,1},{4,6},{5,3},{6,0},{7,5},{8,10},{9,15},{10,... | collective-permute-start | bytes 786440 | tf_op jit(solution)/shard_map/ppermute | solution.py:49
  14.4 11.9 %collective-permute-start.5 = (f32[2,2,128,128]{3,2,1,0:T(8,128)S(1)}, f32[2,2,128,128]{3,2,1,0:T(8,128)S(1)}, u32[]{:S(2)}, u32[]{:S(2)}) collective-permute-start(f32[2,2,128,128]{3,2,1,0:T(8,128)S(1)} %get-tuple-element.44.green1), channel_id=1, source_target_pairs={{1,2},{3,4},{5,6},{2,1},{4,3},{6,5},{9,10},{11,12},{13,14},{10,9},... | collective-permute-start | bytes 786440 | tf_op jit(solution)/shard_map/ppermute | solution.py:29
  24.6 6.4 %collective-permute-start.6 = (f32[2,2,128,128]{3,2,1,0:T(8,128)S(1)}, f32[2,2,128,128]{3,2,1,0:T(8,128)S(1)}, u32[]{:S(2)}, u32[]{:S(2)}) collective-permute-start(f32[2,2,128,128]{3,2,1,0:T(8,128)S(1)} %get-tuple-element.48), channel_id=1, source_target_pairs={{0,1},{1,0},{2,3},{3,2},{4,5},{5,4},{6,7},{7,6},{8,16},{9,17},{10,... | collective-permute-start | bytes 786440 | tf_op jit(solution)/shard_map/ppermute | solution.py:42
  26.2 4.8 %collective-permute-start.7 = (f32[2,2,128,128]{3,2,1,0:T(8,128)S(1)}, f32[2,2,128,128]{3,2,1,0:T(8,128)S(1)}, u32[]{:S(2)}, u32[]{:S(2)}) collective-permute-start(f32[2,2,128,128]{3,2,1,0:T(8,128)S(1)} %get-tuple-element.49), channel_id=1, source_target_pairs={{0,8},{16,24},{8,0},{24,16},{1,9},{17,25},{9,1},{25,17},{2,10},{18... | collective-permute-start | bytes 786440 | tf_op jit(solution)/shard_map/ppermute | solution.py:29
  27.2 7.6 %collective-permute-start.8 = (f32[2,2,128,128]{3,2,1,0:T(8,128)S(1)}, f32[2,2,128,128]{3,2,1,0:T(8,128)S(1)}, u32[]{:S(2)}, u32[]{:S(2)}) collective-permute-start(f32[2,2,128,128]{3,2,1,0:T(8,128)S(1)} %get-tuple-element.53), channel_id=1, source_target_pairs={{0,1},{1,0},{2,3},{3,2},{4,5},{5,4},{6,7},{7,6},{8,16},{9,17},{10,... | collective-permute-start | bytes 786440 | tf_op jit(solution)/shard_map/ppermute | solution.py:42
  30.4 4.4 %collective-permute-start.9 = (f32[2,2,128,128]{3,2,1,0:T(8,128)S(1)}, f32[2,2,128,128]{3,2,1,0:T(8,128)S(1)}, u32[]{:S(2)}, u32[]{:S(2)}) collective-permute-start(f32[2,2,128,128]{3,2,1,0:T(8,128)S(1)} %get-tuple-element.54), channel_id=1, source_target_pairs={{0,8},{16,24},{8,0},{24,16},{1,9},{17,25},{9,1},{25,17},{2,10},{18... | collective-permute-start | bytes 786440 | tf_op jit(solution)/shard_map/ppermute | solution.py:29
  31.0 3.7 %collective-permute-start.12 = (f32[2,128]{1,0:T(2,128)S(1)}, f32[2,128]{1,0:T(2,128)S(1)}, u32[]{:S(2)}, u32[]{:S(2)}) collective-permute-start(f32[2,128]{1,0:T(2,128)S(1)} %get-tuple-element.55.rest_0_), channel_id=1, source_target_pairs={{0,24},{8,0},{16,8},{24,16},{1,25},{9,1},{17,9},{25,17},{2,26},{10... | collective-permute-start | bytes 3080 | tf_op jit(solution)/shard_map/ppermute | solution.py:222
  31.0 3.7 %collective-permute-start.11 = (f32[2,128]{1,0:T(2,128)S(1)}, f32[2,128]{1,0:T(2,128)S(1)}, u32[]{:S(2)}, u32[]{:S(2)}) collective-permute-start(f32[2,128]{1,0:T(2,128)S(1)} %get-tuple-element.55.rest_0_), channel_id=1, source_target_pairs={{0,16},{8,24},{16,0},{24,8},{1,17},{9,25},{17,1},{25,9},{2,18},{10... | collective-permute-start | bytes 3080 | tf_op jit(solution)/shard_map/ppermute | solution.py:222
  32.5 3.0 %collective-permute-start.10 = (f32[2,128]{1,0:T(2,128)S(1)}, f32[2,128]{1,0:T(2,128)S(1)}, u32[]{:S(2)}, u32[]{:S(2)}) collective-permute-start(f32[2,128]{1,0:T(2,128)S(1)} %get-tuple-element.55.rest_0_), channel_id=1, source_target_pairs={{0,8},{8,16},{16,24},{24,0},{1,9},{9,17},{17,25},{25,1},{2,10},{10... | collective-permute-start | bytes 3080 | tf_op jit(solution)/shard_map/ppermute | solution.py:222
